TPU v7x, 32 devices: a whole 2x2x4 slice. The times are simulated.
32 devices in a mesh: groups: 2 (over y), leaf: 4 (over x, core), vec: 4 (over z).
Axes of the slice: x: 2, y: 2, z: 4, core: 2. Of those that a mesh axis runs over, the one named last changes fastest.
Arguments:
- vectors: float32 [16, 65536], P('vec', ('groups', 'leaf')), parts along dimension 1, may hold values from -6 to 6
- coords: float32 [3, 65536], P(None, ('groups', 'leaf')), parts along dimension 1, may hold values from -1 to 1
- weights: float32 [65536], P(('groups', 'leaf')), parts along dimension 0, may hold values from 0.05 to 0.5
- basis: float32 [512, 64, 128], P(('groups', 'leaf')), parts along dimension 0, may hold values from -0.5 to 0.5
- transfer: float32 [8, 64, 64], replicated, may hold values from -0.25 to 0.25
- coupling: float32 [316, 64, 64], replicated, may hold values from -0.0625 to 0.0625
- far_leaf: int32 [512, 316], P(('groups', 'leaf')), parts along dimension 0, may hold values from -1 to 255, as said below
- far_parent: int32 [64, 316], P(('groups', 'leaf')), parts along dimension 0, may hold values from -1 to 31, as said below
- near_leaf: int32 [512, 27], P(('groups', 'leaf')), parts along dimension 0, may hold values from -1 to 255, as said below
Outputs:
- product: float32 [16, 65536], P('vec', ('groups', 'leaf')), parts along dimension 1
There are 2 independent parts, one for each index of `groups`. A program takes and returns all parts, laid end to end along the dimension named above; an argument that names none is the same for every part. Nothing has to cross between parts.
Inputs may be any that keep to these rules, and one draw needn't show every extreme that they name: `far_leaf`: -1 marks an empty slot; a live entry names a leaf among the 64 leaves of the same block of 64 leaves as l or of the block just before or after it. `near_leaf`: -1 marks an empty slot; a live entry names a leaf among the 64 leaves of the same block of 64 leaves as l or of the block just before or after it. `far_parent`: -1 marks an empty slot; a live entry names a parent of the same block of 8 parents as q or of the block just before or after it.
All inputs are finite; a program needn't handle non-finite values.
Results may differ from a plain program's by a relative error of at most 0.0003.
Values sent between devices are 32-bit elements; how exact they have to be, the bound alone decides.
A program may use at most 64 MiB of HBM per device.

v0:
```python
import math

import jax
import jax.numpy as jnp
from jax import lax
from jax.sharding import PartitionSpec as P

HI = lax.Precision.HIGHEST
SOFT_SQ = 0.0001


def with_halo(cells, sides, width):
    for axis, dim in sides:
        count = lax.axis_size(axis)
        ends = count - 1
        head = lax.slice_in_dim(cells, 0, width, axis=dim)
        tail = lax.slice_in_dim(cells, cells.shape[dim] - width, cells.shape[dim], axis=dim)
        cells = jnp.concatenate(
            [
                lax.ppermute(tail, axis, [(i, (i + 1) % count) for i in range(ends)]),
                cells,
                lax.ppermute(head, axis, [((i + 1) % count, i) for i in range(ends)]),
            ],
            axis=dim,
        )
    return cells


def couple(source, lists, coupling):
    count = lists.shape[0]
    blk = math.gcd(count, 8)

    def couple_one(part_lists):
        mask = (part_lists >= 0).astype(coupling.dtype)
        picked = source[jnp.maximum(part_lists, 0)] * mask[:, :, None, None]
        return jnp.einsum("ors,novs->nvr", coupling, picked, precision=HI)

    result = lax.map(couple_one, lists.reshape(count // blk, blk, lists.shape[1]))
    return result.reshape(count, source.shape[1], source.shape[2])


def near_field(target_co, source_co, source_wx, lists):
    count = lists.shape[0]
    width = target_co.shape[2]
    nvec = source_wx.shape[0]
    blk = math.gcd(count, 8)

    def near_one(args):
        tco, part_lists = args
        mask = (part_lists >= 0).astype(source_co.dtype)
        safe = jnp.maximum(part_lists, 0)
        sco = source_co[:, safe]
        swx = source_wx[:, safe]
        diff = tco[:, :, None, :, None] - sco[:, :, :, None, :]
        dist_sq = jnp.sum(diff * diff, axis=0)
        kernel = mask[:, :, None, None] / (4.0 * jnp.pi * jnp.sqrt(dist_sq + SOFT_SQ))
        return jnp.einsum("bkpq,vbkq->vbp", kernel, swx, precision=HI)

    blocks_co = target_co.reshape(3, count // blk, blk, width).transpose(1, 0, 2, 3)
    blocks_lists = lists.reshape(count // blk, blk, lists.shape[1])
    result = lax.map(near_one, (blocks_co, blocks_lists))
    return result.transpose(1, 0, 2, 3).reshape(nvec, count, width)


def body(vectors, coords, weights, basis, transfer, coupling, far_leaf, far_parent, near_leaf):
    nleaf, rank, width = basis.shape
    nvec = vectors.shape[0]
    npar = nleaf // 8
    span = nleaf * width
    first = (lax.axis_index("leaf") - 1) * nleaf
    first_par = (lax.axis_index("leaf") - 1) * npar
    coeff = jnp.einsum("lrp,vlp->lvr", basis, vectors.reshape(nvec, nleaf, width), precision=HI)
    parent = jnp.einsum("jrs,qjvs->qvr", transfer, coeff.reshape(npar, 8, nvec, rank), precision=HI)
    near_parents = with_halo(parent.reshape(npar, nvec * rank), (("leaf", 0),), npar)
    par_local = jnp.where(far_parent >= 0, far_parent - first_par, -1)
    far_par = 0.5 * couple(near_parents.reshape(3 * npar, nvec, rank), par_local, coupling)
    down = jnp.einsum("jsr,qvs->qjvr", transfer, far_par, precision=HI).reshape(nleaf, nvec, rank)
    beside = with_halo(coeff.reshape(nleaf, nvec * rank), (("leaf", 0),), nleaf)
    far_local = jnp.where(far_leaf >= 0, far_leaf - first, -1)
    local = couple(beside.reshape(3 * nleaf, nvec, rank), far_local, coupling) + down
    far_out = jnp.einsum("lrp,lvr->vlp", basis, local, precision=HI)
    weighted = vectors * weights[None, :]
    sources = jnp.concatenate([coords, weighted], axis=0)
    beside_all = with_halo(sources, (("leaf", 1),), span)
    around_co = beside_all[:3].reshape(3, 3 * nleaf, width)
    around_wx = beside_all[3:]
    near_local = jnp.where(near_leaf >= 0, near_leaf - first, -1)
    target_co = coords.reshape(3, nleaf, width)
    near_out = near_field(
        target_co, around_co, around_wx.reshape(nvec, 3 * nleaf, width), near_local
    )
    return (far_out + near_out).reshape(nvec, span)


def solution(mesh):
    in_specs = (
        P("vec", ("groups", "leaf")),
        P(None, ("groups", "leaf")),
        P(("groups", "leaf")),
        P(("groups", "leaf"), None, None),
        P(),
        P(),
        P(("groups", "leaf"), None),
        P(("groups", "leaf"), None),
        P(("groups", "leaf"), None),
    )
    out_specs = P("vec", ("groups", "leaf"))
    return jax.shard_map(body, mesh=mesh, in_specs=in_specs, out_specs=out_specs, check_vma=False)
```

profile of v0, /device:TPU:1, one launch (start us, length us, event | category | flops | bytes accessed | tf_op | source)
XLA Modules:
  0.0 575.0 jit_solution(11205766281055153810)
XLA Ops:
  29.0 9.1 %copy.35 = f32[316,64,64]{0,1,2:T(8,128)} copy(f32[316,64,64]{0,2,1:T(8,128)} %param.18) | data formatting | bytes 10354688 | tf_op jit(solution)/shard_map/while | solution.py:38
  41.1 8.4 %gather_fusion.3 = f32[2528,4,64]{2,1,0:T(4,128)} fusion(f32[24,4,64]{2,1,0:T(4,128)S(1)} %pad_maximum_fusion.3, s32[3072]{0:T(1024)S(1)} %pad_clamp_fusion.2), kind=kCustom, calls=%fused_computation.3 | custom fusion | bytes 5187456 | tf_op jit(solution)/shard_map/while/body/eval_jaxpr/gather | solution.py:35
  55.1 12.1 %fusion.29 = f32[8,4,64,1]{2,0,3,1:T(8,128)S(1)} fusion(f32[8,316,4,64]{1,0,3,2:T(8,128)} %copy.49, f32[8,316]{1,0:T(8,128)S(1)} %compare_convert_fusion, f32[316,64,64]{0,2,1:T(8,128)} %param.18), kind=kOutput, calls=%fused_computation.38 | convolution fusion | flops 497674240 | bytes 7784320 | tf_op jit(solution)/shard_map/while/body/eval_jaxpr/ors,novs->nvr/dot_general | solution.py:36
  67.6 174.8 %while.24 = (s32[]{:T(128)}, f32[8,8,4,64]{3,0,1,2:T(8,128)S(1)}, s32[8,8,316]{2,1,0:T(8,128)S(1)}, f32[192,4,64]{2,1,0:T(4,128)S(1)}, f32[316,64,64]{0,1,2:T(8,128)}, /*index=5*/s32[]{:T(128)}, s32[]{:T(128)}) while((s32[]{:T(128)}, f32[8,8,4,64]{3,0,1,2:T(8,128)S(1)}, s32[8,8,316]{2,1,0:T(8,128)S(1)}, f32[192,4,64]{2,1,0:T(4,128)S(1)}, ...), condition=%wide.region_1.2_spmd, body=%wide.region_0.1_spmd.sunk | while | flops 497682848 | bytes 18248664 | solution.py:38
  67.7 8.4 %gather_fusion = f32[2528,4,64]{2,1,0:T(4,128)} fusion(f32[192,4,64]{2,1,0:T(4,128)S(1)} %get-tuple-element.236, s32[3072]{0:T(1024)S(1)} %pad_clamp_fusion.5), kind=kCustom, calls=%fused_computation.clone.1 | custom fusion | bytes 5187456 | tf_op jit(solution)/shard_map/while/body/eval_jaxpr/gather | solution.py:35
  155.2 8.4 %gather_fusion = f32[2528,4,64]{2,1,0:T(4,128)} fusion(f32[192,4,64]{2,1,0:T(4,128)S(1)} %get-tuple-element.236, s32[3072]{0:T(1024)S(1)} %pad_clamp_fusion.5), kind=kCustom, calls=%fused_computation.clone.1 | custom fusion | bytes 5187456 | tf_op jit(solution)/shard_map/while/body/eval_jaxpr/gather | solution.py:35
  177.0 8.4 %gather_fusion = f32[2528,4,64]{2,1,0:T(4,128)} fusion(f32[192,4,64]{2,1,0:T(4,128)S(1)} %get-tuple-element.236, s32[3072]{0:T(1024)S(1)} %pad_clamp_fusion.5), kind=kCustom, calls=%fused_computation.clone.1 | custom fusion | bytes 5187456 | tf_op jit(solution)/shard_map/while/body/eval_jaxpr/gather | solution.py:35
  244.1 327.5 %while.25 = (s32[]{:T(128)}, f32[8,4,8,128]{3,1,2,0:T(4,128)}, s32[8,8,27]{2,1,0:T(8,128)S(1)}, f32[4,192,128]{2,0,1:T(4,128)S(1)}, f32[8,3,8,128]{3,2,0,1:T(8,128)}, /*index=5*/f32[3,192,128]{2,0,1:T(4,128)S(1)}, s32[]{:T(128)}) while((s32[]{:T(128)}, f32[8,4,8,128]{3,1,2,0:T(4,128)}, s32[8,8,27]{2,1,0:T(8,128)S(1)}, ...), condition=%wide.region_4.5_spmd, body=%wide.region_2.4_spmd.sunk | while | flops 208799360 | bytes 31364120 | solution.py:61
  246.2 16.8 %multiply_reduce_fusion.2 = f32[8,27,128,128]{3,2,1,0:T(8,128)} fusion(f32[3,8,27,128]{3,2,1,0:T(8,128)S(1)} %bitcast.128, f32[3,8,128]{2,1,0:T(8,128)S(1)} %dynamic-slice_bitcast_fusion.2), kind=kLoop, calls=%fused_computation.11.clone.1 | loop fusion | flops 28311552 | bytes 14499840 | tf_op jit(solution)/shard_map/while/body/eval_jaxpr/reduce_sum | solution.py:55
  263.9 21.4 %fusion.55 = f32[8,4,8,128]{3,1,2,0:T(4,128)} fusion(f32[8,4,8,128]{3,1,2,0:T(4,128)} %get-tuple-element.206, s32[]{:T(128)} %get-tuple-element.205, f32[4,8,27,128]{3,0,2,1:T(4,128)S(1)} %bitcast.130, f32[8,27,128,128]{3,2,1,0:T(8,128)} %multiply_reduce_fusion.2, f32[8,27]{1,0:T(8,128)S(1)} %convert_bitcast_fusion.5), kind=kOutput, calls=%fused_computation.18.clone.1 | convolution fusion | flops 180486144 | bytes 14615904 | tf_op jit(solution)/shard_map/while/body/eval_jaxpr/bkpq,vbkq->vbp/dot_general | solution.py:57
  287.1 16.8 %multiply_reduce_fusion.2 = f32[8,27,128,128]{3,2,1,0:T(8,128)} fusion(f32[3,8,27,128]{3,2,1,0:T(8,128)S(1)} %bitcast.128, f32[3,8,128]{2,1,0:T(8,128)S(1)} %dynamic-slice_bitcast_fusion.2), kind=kLoop, calls=%fused_computation.11.clone.1 | loop fusion | flops 28311552 | bytes 14499840 | tf_op jit(solution)/shard_map/while/body/eval_jaxpr/reduce_sum | solution.py:55
  304.8 21.4 %fusion.55 = f32[8,4,8,128]{3,1,2,0:T(4,128)} fusion(f32[8,4,8,128]{3,1,2,0:T(4,128)} %get-tuple-element.206, s32[]{:T(128)} %get-tuple-element.205, f32[4,8,27,128]{3,0,2,1:T(4,128)S(1)} %bitcast.130, f32[8,27,128,128]{3,2,1,0:T(8,128)} %multiply_reduce_fusion.2, f32[8,27]{1,0:T(8,128)S(1)} %convert_bitcast_fusion.5), kind=kOutput, calls=%fused_computation.18.clone.1 | convolution fusion | flops 180486144 | bytes 14615904 | tf_op jit(solution)/shard_map/while/body/eval_jaxpr/bkpq,vbkq->vbp/dot_general | solution.py:57
  328.0 16.8 %multiply_reduce_fusion.2 = f32[8,27,128,128]{3,2,1,0:T(8,128)} fusion(f32[3,8,27,128]{3,2,1,0:T(8,128)S(1)} %bitcast.128, f32[3,8,128]{2,1,0:T(8,128)S(1)} %dynamic-slice_bitcast_fusion.2), kind=kLoop, calls=%fused_computation.11.clone.1 | loop fusion | flops 28311552 | bytes 14499840 | tf_op jit(solution)/shard_map/while/body/eval_jaxpr/reduce_sum | solution.py:55
  345.7 21.4 %fusion.55 = f32[8,4,8,128]{3,1,2,0:T(4,128)} fusion(f32[8,4,8,128]{3,1,2,0:T(4,128)} %get-tuple-element.206, s32[]{:T(128)} %get-tuple-element.205, f32[4,8,27,128]{3,0,2,1:T(4,128)S(1)} %bitcast.130, f32[8,27,128,128]{3,2,1,0:T(8,128)} %multiply_reduce_fusion.2, f32[8,27]{1,0:T(8,128)S(1)} %convert_bitcast_fusion.5), kind=kOutput, calls=%fused_computation.18.clone.1 | convolution fusion | flops 180486144 | bytes 14615904 | tf_op jit(solution)/shard_map/while/body/eval_jaxpr/bkpq,vbkq->vbp/dot_general | solution.py:57
  368.9 16.8 %multiply_reduce_fusion.2 = f32[8,27,128,128]{3,2,1,0:T(8,128)} fusion(f32[3,8,27,128]{3,2,1,0:T(8,128)S(1)} %bitcast.128, f32[3,8,128]{2,1,0:T(8,128)S(1)} %dynamic-slice_bitcast_fusion.2), kind=kLoop, calls=%fused_computation.11.clone.1 | loop fusion | flops 28311552 | bytes 14499840 | tf_op jit(solution)/shard_map/while/body/eval_jaxpr/reduce_sum | solution.py:55
  386.6 21.4 %fusion.55 = f32[8,4,8,128]{3,1,2,0:T(4,128)} fusion(f32[8,4,8,128]{3,1,2,0:T(4,128)} %get-tuple-element.206, s32[]{:T(128)} %get-tuple-element.205, f32[4,8,27,128]{3,0,2,1:T(4,128)S(1)} %bitcast.130, f32[8,27,128,128]{3,2,1,0:T(8,128)} %multiply_reduce_fusion.2, f32[8,27]{1,0:T(8,128)S(1)} %convert_bitcast_fusion.5), kind=kOutput, calls=%fused_computation.18.clone.1 | convolution fusion | flops 180486144 | bytes 14615904 | tf_op jit(solution)/shard_map/while/body/eval_jaxpr/bkpq,vbkq->vbp/dot_general | solution.py:57
  409.8 16.8 %multiply_reduce_fusion.2 = f32[8,27,128,128]{3,2,1,0:T(8,128)} fusion(f32[3,8,27,128]{3,2,1,0:T(8,128)S(1)} %bitcast.128, f32[3,8,128]{2,1,0:T(8,128)S(1)} %dynamic-slice_bitcast_fusion.2), kind=kLoop, calls=%fused_computation.11.clone.1 | loop fusion | flops 28311552 | bytes 14499840 | tf_op jit(solution)/shard_map/while/body/eval_jaxpr/reduce_sum | solution.py:55
  427.5 21.4 %fusion.55 = f32[8,4,8,128]{3,1,2,0:T(4,128)} fusion(f32[8,4,8,128]{3,1,2,0:T(4,128)} %get-tuple-element.206, s32[]{:T(128)} %get-tuple-element.205, f32[4,8,27,128]{3,0,2,1:T(4,128)S(1)} %bitcast.130, f32[8,27,128,128]{3,2,1,0:T(8,128)} %multiply_reduce_fusion.2, f32[8,27]{1,0:T(8,128)S(1)} %convert_bitcast_fusion.5), kind=kOutput, calls=%fused_computation.18.clone.1 | convolution fusion | flops 180486144 | bytes 14615904 | tf_op jit(solution)/shard_map/while/body/eval_jaxpr/bkpq,vbkq->vbp/dot_general | solution.py:57
  450.7 16.8 %multiply_reduce_fusion.2 = f32[8,27,128,128]{3,2,1,0:T(8,128)} fusion(f32[3,8,27,128]{3,2,1,0:T(8,128)S(1)} %bitcast.128, f32[3,8,128]{2,1,0:T(8,128)S(1)} %dynamic-slice_bitcast_fusion.2), kind=kLoop, calls=%fused_computation.11.clone.1 | loop fusion | flops 28311552 | bytes 14499840 | tf_op jit(solution)/shard_map/while/body/eval_jaxpr/reduce_sum | solution.py:55
  468.4 21.4 %fusion.55 = f32[8,4,8,128]{3,1,2,0:T(4,128)} fusion(f32[8,4,8,128]{3,1,2,0:T(4,128)} %get-tuple-element.206, s32[]{:T(128)} %get-tuple-element.205, f32[4,8,27,128]{3,0,2,1:T(4,128)S(1)} %bitcast.130, f32[8,27,128,128]{3,2,1,0:T(8,128)} %multiply_reduce_fusion.2, f32[8,27]{1,0:T(8,128)S(1)} %convert_bitcast_fusion.5), kind=kOutput, calls=%fused_computation.18.clone.1 | convolution fusion | flops 180486144 | bytes 14615904 | tf_op jit(solution)/shard_map/while/body/eval_jaxpr/bkpq,vbkq->vbp/dot_general | solution.py:57
  491.6 16.8 %multiply_reduce_fusion.2 = f32[8,27,128,128]{3,2,1,0:T(8,128)} fusion(f32[3,8,27,128]{3,2,1,0:T(8,128)S(1)} %bitcast.128, f32[3,8,128]{2,1,0:T(8,128)S(1)} %dynamic-slice_bitcast_fusion.2), kind=kLoop, calls=%fused_computation.11.clone.1 | loop fusion | flops 28311552 | bytes 14499840 | tf_op jit(solution)/shard_map/while/body/eval_jaxpr/reduce_sum | solution.py:55
  509.3 21.4 %fusion.55 = f32[8,4,8,128]{3,1,2,0:T(4,128)} fusion(f32[8,4,8,128]{3,1,2,0:T(4,128)} %get-tuple-element.206, s32[]{:T(128)} %get-tuple-element.205, f32[4,8,27,128]{3,0,2,1:T(4,128)S(1)} %bitcast.130, f32[8,27,128,128]{3,2,1,0:T(8,128)} %multiply_reduce_fusion.2, f32[8,27]{1,0:T(8,128)S(1)} %convert_bitcast_fusion.5), kind=kOutput, calls=%fused_computation.18.clone.1 | convolution fusion | flops 180486144 | bytes 14615904 | tf_op jit(solution)/shard_map/while/body/eval_jaxpr/bkpq,vbkq->vbp/dot_general | solution.py:57
  532.5 16.8 %multiply_reduce_fusion.2 = f32[8,27,128,128]{3,2,1,0:T(8,128)} fusion(f32[3,8,27,128]{3,2,1,0:T(8,128)S(1)} %bitcast.128, f32[3,8,128]{2,1,0:T(8,128)S(1)} %dynamic-slice_bitcast_fusion.2), kind=kLoop, calls=%fused_computation.11.clone.1 | loop fusion | flops 28311552 | bytes 14499840 | tf_op jit(solution)/shard_map/while/body/eval_jaxpr/reduce_sum | solution.py:55
  550.2 21.4 %fusion.55 = f32[8,4,8,128]{3,1,2,0:T(4,128)} fusion(f32[8,4,8,128]{3,1,2,0:T(4,128)} %get-tuple-element.206, s32[]{:T(128)} %get-tuple-element.205, f32[4,8,27,128]{3,0,2,1:T(4,128)S(1)} %bitcast.130, f32[8,27,128,128]{3,2,1,0:T(8,128)} %multiply_reduce_fusion.2, f32[8,27]{1,0:T(8,128)S(1)} %convert_bitcast_fusion.5), kind=kOutput, calls=%fused_computation.18.clone.1 | convolution fusion | flops 180486144 | bytes 14615904 | tf_op jit(solution)/shard_map/while/body/eval_jaxpr/bkpq,vbkq->vbp/dot_general | solution.py:57
  (172 shorter events, 213.5 us)
Async XLA Ops:
  0.0 1.6 copy-start
  7.3 31.5 %collective-permute-start.2 = (f32[8,256]{1,0:T(8,128)S(1)}, f32[8,256]{1,0:T(8,128)S(1)}, u32[]{:S(2)}, u32[]{:S(2)}) collective-permute-start(f32[8,256]{1,0:T(8,128)S(1)} %reshape.103), channel_id=1, source_target_pairs={{0,4},{4,8},{8,12},{1,5},{5,9},{9,13},{2,6},{6,10},{10,14},{3,7},{... | collective-permute-start | bytes 24584 | tf_op jit(solution)/shard_map/ppermute | solution.py:20
  11.9 29.2 %collective-permute-start.3 = (f32[8,256]{1,0:T(8,128)S(1)}, f32[8,256]{1,0:T(8,128)S(1)}, u32[]{:S(2)}, u32[]{:S(2)}) collective-permute-start(f32[8,256]{1,0:T(8,128)S(1)} %reshape.103), channel_id=1, source_target_pairs={{4,0},{8,4},{12,8},{5,1},{9,5},{13,9},{6,2},{10,6},{14,10},{7,3},{... | collective-permute-start | bytes 24584 | tf_op jit(solution)/shard_map/ppermute | solution.py:22
  13.9 53.3 %collective-permute-start = (f32[64,256]{1,0:T(8,128)S(1)}, f32[64,256]{1,0:T(8,128)S(1)}, u32[]{:S(2)}, u32[]{:S(2)}) collective-permute-start(f32[64,256]{1,0:T(8,128)S(1)} %reshape.101), channel_id=1, source_target_pairs={{0,4},{4,8},{8,12},{1,5},{5,9},{9,13},{2,6},{6,10},{10,14},{3,7},{... | collective-permute-start | bytes 196616 | tf_op jit(solution)/shard_map/ppermute | solution.py:20
  17.6 49.8 %collective-permute-start.1 = (f32[64,256]{1,0:T(8,128)S(1)}, f32[64,256]{1,0:T(8,128)S(1)}, u32[]{:S(2)}, u32[]{:S(2)}) collective-permute-start(f32[64,256]{1,0:T(8,128)S(1)} %reshape.101), channel_id=1, source_target_pairs={{4,0},{8,4},{12,8},{5,1},{9,5},{13,9},{6,2},{10,6},{14,10},{7,3},{... | collective-permute-start | bytes 196616 | tf_op jit(solution)/shard_map/ppermute | solution.py:22
  22.1 220.6 %collective-permute-start.4 = (f32[7,8192]{1,0:T(8,128)}, f32[7,8192]{1,0:T(8,128)}, u32[]{:S(2)}, u32[]{:S(2)}) collective-permute-start(f32[7,8192]{1,0:T(8,128)} %pad_maximum_fusion.2), channel_id=1, source_target_pairs={{0,4},{4,8},{8,12},{1,5},{5,9},{9,13},{2,6},{6,10},{10,14},{3,7},{... | collective-permute-start | bytes 688136 | tf_op jit(solution)/shard_map/ppermute | solution.py:20
  29.0 9.2 %copy-start.1 = (f32[3,8192]{1,0:T(4,128)S(1)}, f32[3,8192]{1,0:T(4,128)}, u32[]{:S(2)}) copy-start(f32[3,8192]{1,0:T(4,128)} %param.14) | copy-start | bytes 294916
  38.8 203.9 %collective-permute-start.5 = (f32[7,8192]{1,0:T(8,128)}, f32[7,8192]{1,0:T(8,128)}, u32[]{:S(2)}, u32[]{:S(2)}) collective-permute-start(f32[7,8192]{1,0:T(8,128)} %pad_maximum_fusion.2), channel_id=1, source_target_pairs={{4,0},{8,4},{12,8},{5,1},{9,5},{13,9},{6,2},{10,6},{14,10},{7,3},{... | collective-permute-start | bytes 688136 | tf_op jit(solution)/shard_map/ppermute | solution.py:22
  67.6 174.9 %copy-start.2 = (f32[8,64,64]{2,1,0:T(8,128)S(1)}, f32[8,64,64]{2,1,0:T(8,128)}, u32[]{:S(2)}) copy-start(f32[8,64,64]{2,1,0:T(8,128)} %param.17) | copy-start | bytes 393220
where the time goes:
time: 576 us; the launch traced here: 575 us
  matrix products  253 us (44%)
  local copies, waits for them, and re-layouts  161 us (28%)
  other arithmetic  142 us (25%)
  starting transfers between devices  17.7 us (3%)
    dot_general x8, matrix products, near_one(): return jnp.einsum('bkpq,vbkq->vbp', kernel, swx, precision=HI)  171 us
    reduce_sum x8, other arithmetic, near_one(): dist_sq = jnp.sum(diff * diff, axis=0)  134 us
    gather x18, local copies, waits for them, and re-layouts, couple_one(): picked = source[jnp.maximum(part_lists, 0)] * mask[:, :, None, None]  126 us
    dot_general x9, matrix products, couple_one(): return jnp.einsum('ors,novs->nvr', coupling, picked, precision=HI)  72.8 us
    ppermute x3, starting transfers between devices, with_halo(): lax.ppermute(tail, axis, [(i, (i + 1) % count) for i in range(ends)])  11.8 us
  transfers between devices with their start and end apart: 6, of which 0 were waited for; matrix products, arithmetic and copies ran while one was open for 38% of the time, Pallas kernels for 0%

commit v1 on v0

v1 whole, which is shorter than its diff:
```python
import functools
import math

import jax
import jax.numpy as jnp
from jax import lax
from jax.experimental import pallas as pl
from jax.experimental.pallas import tpu as pltpu
from jax.sharding import PartitionSpec as P

SOFT_SQ = 0.0001
F32 = jnp.float32
BF16 = jnp.bfloat16
VMEM_BYTES = 48 * 1024 * 1024
NT = (((1,), (1,)), ((), ()))
NN = (((1,), (0,)), ((), ()))


def split(x):
    hi = x.astype(BF16)
    lo = (x - hi.astype(F32)).astype(BF16)
    return hi, lo


def dot(a, b, dims):
    return lax.dot_general(a, b, dims, preferred_element_type=F32)


def dot3(a, b, dims):
    ahi, alo = split(a)
    bhi, blo = split(b)
    return dot(ahi, bhi, dims) + dot(ahi, blo, dims) + dot(alo, bhi, dims)


def twice_diag(c):
    z = jnp.zeros_like(c)
    return jnp.concatenate(
        [jnp.concatenate([c, z], axis=1), jnp.concatenate([z, c], axis=1)], axis=0
    )


def up_kernel(x_ref, basis_ref, out_ref):
    nleaf, nvec, _ = x_ref.shape
    rank = basis_ref.shape[1]

    def step(leaf, carry):
        x = x_ref[leaf]
        xhi = x.astype(BF16).astype(F32)
        lhs = jnp.concatenate([xhi, x - xhi], axis=0).astype(BF16)
        bhi, blo = split(basis_ref[leaf])
        r = dot(lhs, jnp.concatenate([bhi, blo], axis=0), NT)
        out_ref[leaf] = r[:nvec, :rank] + r[nvec:, :rank] + r[:nvec, rank:]
        return carry

    lax.fori_loop(0, nleaf, step, 0, unroll=8)


def far_kernel(
    left_ref, mid_ref, right_ref, transfer_ref, coupling_ref, idx_ref, basis_ref,
    out_ref, all_ref, src_ref, loc_ref,
):
    nleaf, cols = mid_ref.shape
    nvec = out_ref.shape[0]
    rank = basis_ref.shape[1]
    npair = cols // 128
    nsrc = 3 * nleaf
    npar = nleaf // 8
    rows = idx_ref.shape[1]
    per = idx_ref.shape[2]
    depth = src_ref.shape[0]

    for p in range(npair):
        at = slice(p * 128, (p + 1) * 128)
        all_ref[p, :nleaf] = left_ref[:, at]
        all_ref[p, nleaf : 2 * nleaf] = mid_ref[:, at]
        all_ref[p, 2 * nleaf : nsrc] = right_ref[:, at]
        all_ref[p, nsrc:depth] = jnp.zeros((depth - nsrc, 128), F32)
    par = [jnp.zeros((3 * npar, 128), F32) for _ in range(npair)]
    for j in range(8):
        w = twice_diag(transfer_ref[j])
        for p in range(npair):
            c = all_ref[p, pl.ds(j, 3 * npar, stride=8), :]
            par[p] = par[p] + dot3(c, w, NT)
    for p in range(npair):
        all_ref[p, nsrc : nsrc + 3 * npar] = par[p]
        hi, lo = split(all_ref[p])
        src_ref[:, p * 128 : (p + 1) * 128] = hi
        src_ref[:, cols + p * 128 : cols + (p + 1) * 128] = lo

    lane = lax.broadcasted_iota(jnp.int32, (rows, depth), 1)

    def couple(i, acc):
        acc_a, acc_b = acc
        idx = idx_ref[i]
        hot = [
            jnp.where(idx[:, j : j + 1] == lane, 1.0, 0.0).astype(BF16) for j in range(per)
        ]
        got = dot(jnp.concatenate(hot, axis=0), src_ref[...], NN).astype(BF16)
        for h in range(per // 2):
            whi, wlo = [], []
            for j in (2 * h, 2 * h + 1):
                c = coupling_ref[i * per + j]
                chi, clo = split(twice_diag(c))
                whi.append(chi)
                wlo.append(clo)
            whi = jnp.concatenate(whi, axis=1)
            wlo = jnp.concatenate(wlo, axis=1)
            w = jnp.concatenate([whi, wlo], axis=0)

            def take(start):
                return jnp.concatenate(
                    [
                        jnp.concatenate(
                            [
                                got[j * rows : (j + 1) * rows, start + p * 128 : start + (p + 1) * 128]
                                for j in (2 * h, 2 * h + 1)
                            ],
                            axis=1,
                        )
                        for p in range(npair)
                    ],
                    axis=0,
                )

            acc_a = acc_a + dot(take(0), w, NT)
            acc_b = acc_b + dot(take(cols), whi, NT)
        return acc_a, acc_b

    acc_a, acc_b = lax.fori_loop(
        0,
        idx_ref.shape[0],
        couple,
        (jnp.zeros((npair * rows, 256), F32), jnp.zeros((npair * rows, 128), F32)),
    )
    total = acc_a[:, :128] + acc_a[:, 128:] + acc_b
    for p in range(npair):
        loc_ref[p] = total[p * rows : p * rows + nleaf]
    for j in range(8):
        w = twice_diag(transfer_ref[j])
        for p in range(npair):
            far = 0.5 * total[p * rows + nleaf : p * rows + nleaf + npar]
            at = (p, pl.ds(j, npar, stride=8), slice(None))
            loc_ref[at] = loc_ref[at] + dot3(far, w, NN)

    low = lax.broadcasted_iota(jnp.int32, (1, 128), 1) < rank

    def leaf_out(leaf, carry):
        parts = []
        for p in range(npair):
            piece = loc_ref[p, pl.ds(leaf, 1), :]
            parts.append(jnp.where(low, piece, 0.0))
            parts.append(jnp.where(low, 0.0, piece))
        lhs = jnp.concatenate(parts, axis=0)
        lhi = lhs.astype(BF16).astype(F32)
        lhs = jnp.concatenate([lhi, lhs - lhi], axis=0).astype(BF16)
        bhi, blo = split(basis_ref[leaf])
        b = jnp.concatenate([bhi, blo], axis=1)
        r = dot(lhs, jnp.concatenate([b, b], axis=0), NN)
        out_ref[:, pl.ds(pl.multiple_of(leaf * 128, 128), 128)] = (
            r[:nvec, :128] + r[nvec:, :128] + r[:nvec, 128:]
        )
        return carry

    lax.fori_loop(0, nleaf, leaf_out, 0, unroll=8)


def near_kernel(
    list_ref, co_l, co_m, co_r, wx_l, wx_m, wx_r, out_ref, co_ref, wx_ref, tgt_ref, sem
):
    nleaf = co_m.shape[0]
    count = out_ref.shape[0]
    nvec = out_ref.shape[1]
    copies = []
    for n, (src, dst) in enumerate(
        ((co_l, co_ref), (co_m, co_ref), (co_r, co_ref), (wx_l, wx_ref), (wx_m, wx_ref), (wx_r, wx_ref))
    ):
        copies.append(
            pltpu.make_async_copy(src, dst.at[pl.ds((n % 3) * nleaf, nleaf)], sem.at[n])
        )
        copies[-1].start()
    co_ref[3 * nleaf] = jnp.zeros(co_ref.shape[1:], F32)
    wx_ref[3 * nleaf] = jnp.zeros(wx_ref.shape[1:], F32)
    for c in copies:
        c.wait()

    def target(t, carry):
        own = co_ref[list_ref[t, 29]]
        for c in range(3):
            tgt_ref[c] = jnp.broadcast_to(own[c : c + 1], (128, 128)).T

        def pair(k, acc):
            his, los, ws = [], [], []
            for s in range(2):
                m = list_ref[t, 2 * k + s]
                co = co_ref[m]
                d0 = tgt_ref[0] - co[0:1]
                d1 = tgt_ref[1] - co[1:2]
                d2 = tgt_ref[2] - co[2:3]
                kern = lax.rsqrt(d0 * d0 + d1 * d1 + (d2 * d2 + SOFT_SQ))
                hi, lo = split(kern)
                his.append(hi)
                los.append(lo)
                whi, wlo = split(wx_ref[m])
                ws.append(jnp.concatenate([whi, wlo], axis=0))
            rhs = jnp.concatenate(
                [jnp.concatenate(his, axis=1), jnp.concatenate(los, axis=1)], axis=0
            )
            return acc + dot(jnp.concatenate(ws, axis=1), rhs, NT)

        acc = lax.fori_loop(0, list_ref[t, 28], pair, jnp.zeros((2 * nvec, 256), F32))
        out_ref[t] = acc[:nvec, :128] + acc[nvec:, :128] + acc[:nvec, 128:]
        return carry

    lax.fori_loop(0, count, target, 0)


def shift_both(x, axis):
    ends = lax.axis_size(axis) - 1
    from_left = lax.ppermute(x, axis, [(i, i + 1) for i in range(ends)])
    from_right = lax.ppermute(x, axis, [(i + 1, i) for i in range(ends)])
    return from_left, from_right


def body(vectors, coords, weights, basis, transfer, coupling, far_leaf, far_parent, near_leaf):
    nleaf, rank, width = basis.shape
    nvec = vectors.shape[0]
    npar = nleaf // 8
    noff = coupling.shape[0]
    nz = lax.axis_size("vec")
    vec = lax.axis_index("vec")
    first = (lax.axis_index("leaf") - 1) * nleaf
    first_par = (lax.axis_index("leaf") - 1) * npar
    count = nleaf // nz
    nall = nvec * nz
    slots = near_leaf.shape[1]

    leaf_x = vectors.reshape(nvec, nleaf, width).transpose(1, 0, 2)
    leaf_w = (weights * (1.0 / (4.0 * math.pi))).reshape(nleaf, 1, width)
    wx = lax.all_gather(leaf_x * leaf_w, "vec", axis=1, tiled=True)
    co = jnp.pad(coords.reshape(3, nleaf, width).transpose(1, 0, 2), ((0, 0), (0, 5), (0, 0)))
    co_l, co_r = shift_both(co, "leaf")

    params = pltpu.CompilerParams(vmem_limit_bytes=VMEM_BYTES)
    coeff = pl.pallas_call(
        up_kernel,
        out_shape=jax.ShapeDtypeStruct((nleaf, nvec, rank), F32),
        compiler_params=params,
        name="up",
        cost_estimate=pl.CostEstimate(flops=10**8, bytes_accessed=4 * 10**6, transcendentals=0),
    )(leaf_x, basis)
    coeff = coeff.reshape(nleaf, nvec * rank)
    c_l, c_r = shift_both(coeff, "leaf")
    wx_l, wx_r = shift_both(wx, "leaf")

    per = 4
    rows = -(-(nleaf + npar) // 16) * 16
    idx = jnp.concatenate(
        [
            jnp.where(far_leaf >= 0, far_leaf - first, -1),
            jnp.where(far_parent >= 0, far_parent - first_par + 3 * nleaf, -1),
            jnp.full((rows - nleaf - npar, noff), -1, jnp.int32),
        ],
        axis=0,
    )
    idx = idx.reshape(rows, noff // per, per).transpose(1, 0, 2)
    depth = 256
    cols = nvec * rank
    far_out = pl.pallas_call(
        far_kernel,
        out_shape=jax.ShapeDtypeStruct((nvec, nleaf * width), F32),
        scratch_shapes=[
            pltpu.VMEM((cols // 128, depth, 128), F32),
            pltpu.VMEM((depth, 2 * cols), BF16),
            pltpu.VMEM((cols // 128, nleaf, 128), F32),
        ],
        compiler_params=params,
        name="far",
        cost_estimate=pl.CostEstimate(flops=10**10, bytes_accessed=10**8, transcendentals=0),
    )(c_l, coeff, c_r, transfer, coupling, idx, basis)

    mine = lax.dynamic_slice_in_dim(near_leaf, vec * count, count, axis=0)
    live = mine >= 0
    at = jnp.arange(slots)
    place = jnp.sum(live[:, None, :] & (at[None, None, :] < at[None, :, None]), axis=2)
    empty = 3 * nleaf
    j = jnp.arange(28)
    lists = empty + jnp.sum(
        jnp.where(
            live[:, None, :] & (place[:, None, :] == j[None, :, None]),
            (mine - first - empty)[:, None, :],
            0,
        ),
        axis=2,
    )
    pairs = (jnp.sum(live, axis=1) + 1) // 2
    own = nleaf + vec * count + jnp.arange(count)
    lists = jnp.concatenate([lists, pairs[:, None], own[:, None]], axis=1).astype(jnp.int32)
    anywhere = pl.BlockSpec(memory_space=pl.ANY)
    near = pl.pallas_call(
        near_kernel,
        out_shape=jax.ShapeDtypeStruct((count, nall, width), F32),
        in_specs=[pl.BlockSpec(memory_space=pltpu.SMEM)] + [anywhere] * 6,
        scratch_shapes=[
            pltpu.VMEM((3 * nleaf + 1, 8, width), F32),
            pltpu.VMEM((3 * nleaf + 1, nall, width), F32),
            pltpu.VMEM((3, width, width), F32),
            pltpu.SemaphoreType.DMA((6,)),
        ],
        compiler_params=params,
        name="near",
        cost_estimate=pl.CostEstimate(flops=10**10, bytes_accessed=10**8, transcendentals=0),
    )(lists, co_l, co, co_r, wx_l, wx, wx_r)
    near = lax.all_to_all(near, "vec", split_axis=1, concat_axis=0, tiled=True)
    return far_out + near.transpose(1, 0, 2).reshape(nvec, nleaf * width)


def solution(mesh):
    in_specs = (
        P("vec", ("groups", "leaf")),
        P(None, ("groups", "leaf")),
        P(("groups", "leaf")),
        P(("groups", "leaf"), None, None),
        P(),
        P(),
        P(("groups", "leaf"), None),
        P(("groups", "leaf"), None),
        P(("groups", "leaf"), None),
    )
    out_specs = P("vec", ("groups", "leaf"))
    return jax.shard_map(body, mesh=mesh, in_specs=in_specs, out_specs=out_specs, check_vma=False)
```

time: 576 us -> 158 us (0.27)
  matrix products: 253 us -> 0 us
  other arithmetic: 142 us -> 3.5 us
  local copies, waits for them, and re-layouts: 161 us -> 25.3 us
  Pallas kernels: 0 us -> 89.2 us
  blocking collectives: 0 us -> 15.1 us
    dot_general x21 -> x0, matrix products: 253 us -> none  [the longest x8 171 us: near_one(): return jnp.einsum('bkpq,vbkq->vbp', kernel, swx, precision=HI)]
    gather x42 -> x0, local copies, waits for them, and re-layouts: 141 us -> none  [the longest x18 126 us: couple_one(): picked = source[jnp.maximum(part_lists, 0)] * mask[:, :, None, None]]
    reduce_sum x8 -> x3, other arithmetic: 134 us -> 0.89 us  [the longest x1 0.55 us: body(): jnp.sum(live[:, None, :] & (at[None, None, :] < at[None, :, None]), axis=2)]
    pallas_call x0 -> x3, Pallas kernels: none -> 89.2 us  [the longest x1 44.4 us: body(): pl.pallas_call(far_kernel, out_shape=jax.ShapeDtypeStruct((nvec, nleaf *...]
    unnamed x7 -> x15, local copies, waits for them, and re-layouts: 2.25 us -> 17.5 us
    all_gather x0 -> x1, blocking collectives: none -> 15.1 us  [body(): wx = lax.all_gather(leaf_x * leaf_w, 'vec', axis=1, tiled=True)]
    while x1 -> x0, local copies, waits for them, and re-layouts: 9.13 us -> none  [couple(): lax.map(couple_one, lists.reshape(count // blk, blk, lists.shape[1]))]
  transfers between devices with their start and end apart: 6 -> 7, of which waited for: 0 -> 0; matrix products, arithmetic and copies ran while one was open for 38% -> 13% of each run, Pallas kernels for 0% -> 57%
where the time goes in v1:
time: 158 us; the launch traced here: 157 us
  Pallas kernels  89.2 us (56%)
  local copies, waits for them, and re-layouts  25.3 us (16%)
  starting transfers between devices  23.2 us (15%)
  blocking collectives  15.1 us (10%)
  other arithmetic  3.5 us (2%)
    pallas_call x1, Pallas kernels, body(): pl.pallas_call(far_kernel, out_shape=jax.ShapeDtypeStruct((nvec, nleaf *...  44.4 us
    pallas_call x1, Pallas kernels, body(): pl.pallas_call(near_kernel, out_shape=jax.ShapeDtypeStruct((count, nall,...  42.3 us
    unnamed x15, local copies, waits for them, and re-layouts  17.5 us
    all_gather x1, blocking collectives, body(): wx = lax.all_gather(leaf_x * leaf_w, 'vec', axis=1, tiled=True)  15.1 us
    ppermute x3, starting transfers between devices, shift_both(): from_left = lax.ppermute(x, axis, [(i, i + 1) for i in range(ends)])  12.3 us
    ppermute x3, starting transfers between devices, shift_both(): from_right = lax.ppermute(x, axis, [(i + 1, i) for i in range(ends)])  5.76 us
    all_to_all x1, starting transfers between devices, body(): near = lax.all_to_all(near, 'vec', split_axis=1, concat_axis=0, tiled=True)  5.1 us
  transfers between devices with their start and end apart: 7, of which 0 were waited for; matrix products, arithmetic and copies ran while one was open for 13% of the time, Pallas kernels for 57%

profile of v1, /device:TPU:1, one launch (start us, length us, event | category | flops | bytes accessed | tf_op | source)
XLA Modules:
  0.0 156.5 jit_solution(8841350267825035026)
XLA Ops:
  0.0 0.9 pad.4.co_m
  0.9 4.5 %collective-permute-start.2 = (f32[64,8,128]{2,1,0:T(8,128)S(1)}, f32[64,8,128]{2,1,0:T(8,128)}, u32[]{:S(2)}, u32[]{:S(2)}) collective-permute-start(f32[64,8,128]{2,1,0:T(8,128)S(1)} %pad.4.co_m), channel_id=1, source_target_pairs={{0,4},{4,8},{8,12},{1,5},{5,9},{9,13},{2,6},{6,10},{10,14},{3,7},{... | collective-permute-start | bytes 786440 | tf_op jit(solution)/shard_map/ppermute | solution.py:219
  5.4 1.9 %collective-permute-start.3 = (f32[64,8,128]{2,1,0:T(8,128)S(1)}, f32[64,8,128]{2,1,0:T(8,128)}, u32[]{:S(2)}, u32[]{:S(2)}) collective-permute-start(f32[64,8,128]{2,1,0:T(8,128)S(1)} %pad.4.co_m), channel_id=1, source_target_pairs={{4,0},{8,4},{12,8},{5,1},{9,5},{13,9},{6,2},{10,6},{14,10},{7,3},{... | collective-permute-start | bytes 786440 | tf_op jit(solution)/shard_map/ppermute | solution.py:220
  7.4 0.8 multiply_bitcast_fusion
  8.1 0.9 broadcast_multiply_fusion
  9.1 15.1 %all_gather.3 = f32[64,16,128]{2,0,1:T(8,128)S(1)} all-gather(f32[64,4,128]{2,0,1:T(8,128)S(1)} %copy.68), channel_id=1, replica_groups=mesh['groups'=2,'leaf'=4,'vec'=4] {'vec'}, dimensions={1}, use_global_device_ids=true | all-gather | bytes 655360 | tf_op jit(solution)/shard_map/all_gather | solution.py:239
  24.2 1.1 copy.69.wx_m
  25.3 4.2 %collective-permute-start.4 = (f32[64,16,128]{2,1,0:T(8,128)}, f32[64,16,128]{2,1,0:T(8,128)}, u32[]{:S(2)}, u32[]{:S(2)}) collective-permute-start(f32[64,16,128]{2,1,0:T(8,128)} %copy.69.wx_m), channel_id=1, source_target_pairs={{0,4},{4,8},{8,12},{1,5},{5,9},{9,13},{2,6},{6,10},{10,14},{3,7},{... | collective-permute-start | bytes 1572872 | tf_op jit(solution)/shard_map/ppermute | solution.py:219
  29.5 1.9 %collective-permute-start.5 = (f32[64,16,128]{2,1,0:T(8,128)}, f32[64,16,128]{2,1,0:T(8,128)}, u32[]{:S(2)}, u32[]{:S(2)}) collective-permute-start(f32[64,16,128]{2,1,0:T(8,128)} %copy.69.wx_m), channel_id=1, source_target_pairs={{4,0},{8,4},{12,8},{5,1},{9,5},{13,9},{6,2},{10,6},{14,10},{7,3},{... | collective-permute-start | bytes 1572872 | tf_op jit(solution)/shard_map/ppermute | solution.py:220
  31.5 1.6 %copy-done = f32[64,64,128]{2,1,0:T(8,128)S(1)} copy-done((f32[64,64,128]{2,1,0:T(8,128)S(1)}, f32[64,64,128]{2,1,0:T(8,128)}, u32[]{:S(2)}) %copy-start) | copy-done | bytes 2097176
  33.1 0.9 copy-done.2
  34.0 2.5 %up.1 = f32[64,4,64]{2,1,0:T(4,128)S(1)} custom-call(f32[64,4,128]{2,1,0:T(4,128)S(1)} %bitcast.24, f32[64,64,128]{2,1,0:T(8,128)S(1)} %copy-done), custom_call_target="tpu_custom_call" | custom-call | flops 100000000 | bytes 4000000 | tf_op jit(solution)/shard_map/up/pallas_call | solution.py:244
  36.5 0.8 reshape.97.mid_ref
  37.3 3.6 %collective-permute-start = (f32[64,256]{1,0:T(8,128)}, f32[64,256]{1,0:T(8,128)}, u32[]{:S(2)}, u32[]{:S(2)}) collective-permute-start(f32[64,256]{1,0:T(8,128)} %reshape.97.mid_ref), channel_id=1, source_target_pairs={{0,4},{4,8},{8,12},{1,5},{5,9},{9,13},{2,6},{6,10},{10,14},{3,7},{... | collective-permute-start | bytes 196616 | tf_op jit(solution)/shard_map/ppermute | solution.py:219
  41.0 12.4 %copy.62.coupling_ref = f32[316,64,64]{2,1,0:T(8,128)} copy(f32[316,64,64]{0,2,1:T(8,128)} %param.14) | data formatting | bytes 10354688 | tf_op args[5]
  54.3 2.3 %copy.61 = s32[80,79,4]{2,0,1:T(8,128)S(1)} copy(s32[80,79,4]{0,2,1:T(4,128)} %reshape.98) | data formatting | bytes 202240 | tf_op jit(solution)/shard_map/reshape | solution.py:265
  57.8 1.9 %collective-permute-start.1 = (f32[64,256]{1,0:T(8,128)}, f32[64,256]{1,0:T(8,128)}, u32[]{:S(2)}, u32[]{:S(2)}) collective-permute-start(f32[64,256]{1,0:T(8,128)} %reshape.97.mid_ref), channel_id=1, source_target_pairs={{4,0},{8,4},{12,8},{5,1},{9,5},{13,9},{6,2},{10,6},{14,10},{7,3},{... | collective-permute-start | bytes 196616 | tf_op jit(solution)/shard_map/ppermute | solution.py:220
  59.8 42.3 %near.1 = f32[16,16,128]{2,1,0:T(8,128)S(1)} custom-call(s32[16,30]{1,0:T(8,128)S(1)} %pad_add_fusion.1.list_ref, f32[64,8,128]{2,1,0:T(8,128)} %collective-permute-done.2.co_l, f32[64,8,128]{2,1,0:T(8,128)S(1)} %pad.4.co_m, f32[64,8,128]{2,1,0:T(8,128)} %collective-permute-done.3.co_r, f32[64,16,128]{2,1,0:T(8,128)} %collective-permute-done.4.wx_l, ...), custom_call_target="tpu_custom_call" | custom-call | flops 10000000000 | bytes 100000000 | tf_op jit(solution)/shard_map/near/pallas_call | solution.py:299
  102.8 5.1 %all-to-all-start = ((f32[16,16,128]{2,0,1:T(8,128)}), f32[16,16,128]{2,0,1:T(8,128)}, u32[]{:S(2)}, u32[]{:S(2)}) async-start(f32[16,16,128]{2,0,1:T(8,128)} %copy.72), calls=%async_computation | async-start | bytes 262144 | tf_op jit(solution)/shard_map/all_to_all | solution.py:313
  107.9 1.6 %copy-done.1 = f32[64,64,128]{2,1,0:T(8,128)S(1)} copy-done((f32[64,64,128]{2,1,0:T(8,128)S(1)}, f32[64,64,128]{2,1,0:T(8,128)}, u32[]{:S(2)}) %copy-start.1) | copy-done | bytes 2097176
  109.5 0.9 copy-done.3
  110.4 44.4 %far.1 = f32[4,8192]{1,0:T(4,128)S(1)} custom-call(f32[64,256]{1,0:T(8,128)} %collective-permute-done.left_ref, f32[64,256]{1,0:T(8,128)} %reshape.97.mid_ref, f32[64,256]{1,0:T(8,128)} %collective-permute-done.1.right_ref, f32[8,64,64]{2,1,0:T(8,128)S(1)} %copy-done.3, f32[316,64,64]{2,1,0:T(8,128)} %copy.62.coupling_ref, s32[79,80,4]{2,1,0:T(8,128)S(1)} %bitcast.23, ...), custom_call_target="tpu_custom_call" | custom-call | flops 10000000000 | bytes 100000000 | tf_op jit(solution)/shard_map/far/pallas_call | solution.py:268
  154.9 0.9 copy.73
  155.8 0.8 bitcast_add_fusion
  (35 shorter events, 2.8 us)
Async XLA Ops:
  0.9 56.9 %collective-permute-start.2 = (f32[64,8,128]{2,1,0:T(8,128)S(1)}, f32[64,8,128]{2,1,0:T(8,128)}, u32[]{:S(2)}, u32[]{:S(2)}) collective-permute-start(f32[64,8,128]{2,1,0:T(8,128)S(1)} %pad.4.co_m), channel_id=1, source_target_pairs={{0,4},{4,8},{8,12},{1,5},{5,9},{9,13},{2,6},{6,10},{10,14},{3,7},{... | collective-permute-start | bytes 786440 | tf_op jit(solution)/shard_map/ppermute | solution.py:219
  5.4 54.3 %collective-permute-start.3 = (f32[64,8,128]{2,1,0:T(8,128)S(1)}, f32[64,8,128]{2,1,0:T(8,128)}, u32[]{:S(2)}, u32[]{:S(2)}) collective-permute-start(f32[64,8,128]{2,1,0:T(8,128)S(1)} %pad.4.co_m), channel_id=1, source_target_pairs={{4,0},{8,4},{12,8},{5,1},{9,5},{13,9},{6,2},{10,6},{14,10},{7,3},{... | collective-permute-start | bytes 786440 | tf_op jit(solution)/shard_map/ppermute | solution.py:220
  25.3 34.4 %collective-permute-start.4 = (f32[64,16,128]{2,1,0:T(8,128)}, f32[64,16,128]{2,1,0:T(8,128)}, u32[]{:S(2)}, u32[]{:S(2)}) collective-permute-start(f32[64,16,128]{2,1,0:T(8,128)} %copy.69.wx_m), channel_id=1, source_target_pairs={{0,4},{4,8},{8,12},{1,5},{5,9},{9,13},{2,6},{6,10},{10,14},{3,7},{... | collective-permute-start | bytes 1572872 | tf_op jit(solution)/shard_map/ppermute | solution.py:219
  29.5 30.3 %collective-permute-start.5 = (f32[64,16,128]{2,1,0:T(8,128)}, f32[64,16,128]{2,1,0:T(8,128)}, u32[]{:S(2)}, u32[]{:S(2)}) collective-permute-start(f32[64,16,128]{2,1,0:T(8,128)} %copy.69.wx_m), channel_id=1, source_target_pairs={{4,0},{8,4},{12,8},{5,1},{9,5},{13,9},{6,2},{10,6},{14,10},{7,3},{... | collective-permute-start | bytes 1572872 | tf_op jit(solution)/shard_map/ppermute | solution.py:220
  31.5 1.6 %copy-start = (f32[64,64,128]{2,1,0:T(8,128)S(1)}, f32[64,64,128]{2,1,0:T(8,128)}, u32[]{:S(2)}) copy-start(f32[64,64,128]{2,1,0:T(8,128)} %basis_ref.3) | copy-start | bytes 6291460
  33.1 0.9 copy-start.2
  37.3 70.6 %collective-permute-start = (f32[64,256]{1,0:T(8,128)}, f32[64,256]{1,0:T(8,128)}, u32[]{:S(2)}, u32[]{:S(2)}) collective-permute-start(f32[64,256]{1,0:T(8,128)} %reshape.97.mid_ref), channel_id=1, source_target_pairs={{0,4},{4,8},{8,12},{1,5},{5,9},{9,13},{2,6},{6,10},{10,14},{3,7},{... | collective-permute-start | bytes 196616 | tf_op jit(solution)/shard_map/ppermute | solution.py:219
  40.9 12.4 %copy-start.6 = (s32[8,316]{1,0:T(8,128)S(1)}, s32[8,316]{1,0:T(8,128)}, u32[]{:S(2)}) copy-start(s32[8,316]{1,0:T(8,128)} %param.16) | copy-start | bytes 30340
  40.9 12.4 %copy-start.4 = (s32[64,316]{1,0:T(8,128)S(1)}, s32[64,316]{1,0:T(8,128)}, u32[]{:S(2)}) copy-start(s32[64,316]{1,0:T(8,128)} %param.15) | copy-start | bytes 242692
  41.0 15.7 %copy-start.5 = (s32[64,27]{0,1:T(8,128)S(1)}, s32[64,27]{0,1:T(8,128)}, u32[]{:S(2)}) copy-start(s32[64,27]{0,1:T(8,128)} %param.17) | copy-start | bytes 20740
  57.8 50.1 %collective-permute-start.1 = (f32[64,256]{1,0:T(8,128)}, f32[64,256]{1,0:T(8,128)}, u32[]{:S(2)}, u32[]{:S(2)}) collective-permute-start(f32[64,256]{1,0:T(8,128)} %reshape.97.mid_ref), channel_id=1, source_target_pairs={{4,0},{8,4},{12,8},{5,1},{9,5},{13,9},{6,2},{10,6},{14,10},{7,3},{... | collective-permute-start | bytes 196616 | tf_op jit(solution)/shard_map/ppermute | solution.py:220
  102.8 52.1 %all-to-all-start = ((f32[16,16,128]{2,0,1:T(8,128)}), f32[16,16,128]{2,0,1:T(8,128)}, u32[]{:S(2)}, u32[]{:S(2)}) async-start(f32[16,16,128]{2,0,1:T(8,128)} %copy.72), calls=%async_computation | async-start | bytes 262144 | tf_op jit(solution)/shard_map/all_to_all | solution.py:313
  107.9 1.6 %copy-start.1 = (f32[64,64,128]{2,1,0:T(8,128)S(1)}, f32[64,64,128]{2,1,0:T(8,128)}, u32[]{:S(2)}) copy-start(f32[64,64,128]{2,1,0:T(8,128)} %basis_ref.3) | copy-start | bytes 6291460
  109.5 0.9 copy-start.3

commit v2 on v1

--- a/solution.py
+++ b/solution.py
@@ -11,6 +11,8 @@
 SOFT_SQ = 0.0001
 F32 = jnp.float32
 BF16 = jnp.bfloat16
+FAR_STEP = 32
+NEAR_STEP = 4
 VMEM_BYTES = 48 * 1024 * 1024
 NT = (((1,), (1,)), ((), ()))
 NN = (((1,), (0,)), ((), ()))
@@ -56,8 +58,8 @@
 
 
 def far_kernel(
-    left_ref, mid_ref, right_ref, transfer_ref, coupling_ref, idx_ref, basis_ref,
-    out_ref, all_ref, src_ref, loc_ref,
+    left_ref, mid_ref, right_ref, transfer_ref, coupling_ref, leaf_ref, parent_ref, basis_ref,
+    out_ref, all_ref, src_ref, loc_ref, idx_ref, wide_ref,
 ):
     nleaf, cols = mid_ref.shape
     nvec = out_ref.shape[0]
@@ -66,8 +68,31 @@
     nsrc = 3 * nleaf
     npar = nleaf // 8
     rows = idx_ref.shape[1]
-    per = idx_ref.shape[2]
+    noff = coupling_ref.shape[2]
+    per = FAR_STEP
     depth = src_ref.shape[0]
+
+    def widen(r, carry):
+        m = coupling_ref[r]
+        wide_ref[pl.ds(r, noff, stride=rank), :] = jnp.concatenate([m, m], axis=0).T
+        return carry
+
+    lax.fori_loop(0, rank, widen, 0, unroll=4)
+    spare = wide_ref.shape[0] - noff * rank
+    wide_ref[noff * rank :] = jnp.zeros((spare, 128), F32)
+
+    first = (lax.axis_index("leaf") - 1) * nleaf
+    first_par = (lax.axis_index("leaf") - 1) * npar
+    for b in range(-(-noff // 128)):
+        at = slice(b * 128, min(noff, (b + 1) * 128))
+        width = at.stop - at.start
+        lists = leaf_ref[:, at]
+        parents = parent_ref[:, at]
+        idx_ref[b] = jnp.full((rows, 128), -1, jnp.int32)
+        idx_ref[b, :nleaf, :width] = jnp.where(lists >= 0, lists - first, -1)
+        idx_ref[b, nleaf : nleaf + npar, :width] = jnp.where(
+            parents >= 0, parents - first_par + nsrc, -1
+        )
 
     for p in range(npair):
         at = slice(p * 128, (p + 1) * 128)
@@ -88,51 +113,46 @@
         src_ref[:, cols + p * 128 : cols + (p + 1) * 128] = lo
 
     lane = lax.broadcasted_iota(jnp.int32, (rows, depth), 1)
-
-    def couple(i, acc):
-        acc_a, acc_b = acc
-        idx = idx_ref[i]
+    low = lax.broadcasted_iota(jnp.int32, (1, 128), 1) < rank
+
+    def block_pair(o):
+        c = [wide_ref[pl.ds(pl.multiple_of((o + k) * rank, rank), rank), :] for k in range(2)]
+        return split(jnp.where(low, c[0], c[1]))
+
+    def couple(b, i, acc):
+        idx = pltpu.roll(idx_ref[b], (128 - per * i) % 128, 1)
         hot = [
             jnp.where(idx[:, j : j + 1] == lane, 1.0, 0.0).astype(BF16) for j in range(per)
         ]
         got = dot(jnp.concatenate(hot, axis=0), src_ref[...], NN).astype(BF16)
-        for h in range(per // 2):
-            whi, wlo = [], []
-            for j in (2 * h, 2 * h + 1):
-                c = coupling_ref[i * per + j]
-                chi, clo = split(twice_diag(c))
-                whi.append(chi)
-                wlo.append(clo)
-            whi = jnp.concatenate(whi, axis=1)
-            wlo = jnp.concatenate(wlo, axis=1)
-            w = jnp.concatenate([whi, wlo], axis=0)
-
-            def take(start):
-                return jnp.concatenate(
-                    [
-                        jnp.concatenate(
-                            [
-                                got[j * rows : (j + 1) * rows, start + p * 128 : start + (p + 1) * 128]
-                                for j in (2 * h, 2 * h + 1)
-                            ],
-                            axis=1,
-                        )
-                        for p in range(npair)
-                    ],
-                    axis=0,
+        w = [block_pair(b * 128 + i * per + j) for j in range(0, per, 2)]
+        w = [jnp.concatenate([x[n] for x in w], axis=1) for n in range(2)]
+        lhs = []
+        for p in range(2 * npair):
+            for v in range(2):
+                at = slice(p * 128 + v * rank, p * 128 + (v + 1) * rank)
+                lhs.append(
+                    jnp.concatenate(
+                        [got[j * rows : (j + 1) * rows, at] for j in range(per)], axis=1
+                    )
                 )
-
-            acc_a = acc_a + dot(take(0), w, NT)
-            acc_b = acc_b + dot(take(cols), whi, NT)
-        return acc_a, acc_b
-
-    acc_a, acc_b = lax.fori_loop(
-        0,
-        idx_ref.shape[0],
-        couple,
-        (jnp.zeros((npair * rows, 256), F32), jnp.zeros((npair * rows, 128), F32)),
+        return acc + dot(jnp.concatenate(lhs, axis=0), jnp.concatenate(w, axis=0), NT)
+
+    acc = jnp.zeros((2 * nvec * rows, 2 * rank), F32)
+    for b in range(-(-noff // 128)):
+        steps = -(-min(128, noff - b * 128) // per)
+        acc = lax.fori_loop(0, steps, functools.partial(couple, b), acc, unroll=1)
+    hi_part, lo_part = acc[: nvec * rows], acc[nvec * rows :]
+    total = hi_part[:, :rank] + hi_part[:, rank:] + lo_part[:, :rank]
+    total = jnp.concatenate(
+        [
+            jnp.concatenate(
+                [total[v * rows : (v + 1) * rows] for v in (2 * p, 2 * p + 1)], axis=1
+            )
+            for p in range(npair)
+        ],
+        axis=0,
     )
-    total = acc_a[:, :128] + acc_a[:, 128:] + acc_b
     for p in range(npair):
         loc_ref[p] = total[p * rows : p * rows + nleaf]
     for j in range(8):
@@ -141,8 +161,6 @@
             far = 0.5 * total[p * rows + nleaf : p * rows + nleaf + npar]
             at = (p, pl.ds(j, npar, stride=8), slice(None))
             loc_ref[at] = loc_ref[at] + dot3(far, w, NN)
-
-    low = lax.broadcasted_iota(jnp.int32, (1, 128), 1) < rank
 
     def leaf_out(leaf, carry):
         parts = []
@@ -168,8 +186,9 @@
     list_ref, co_l, co_m, co_r, wx_l, wx_m, wx_r, out_ref, co_ref, wx_ref, tgt_ref, sem
 ):
     nleaf = co_m.shape[0]
-    count = out_ref.shape[0]
-    nvec = out_ref.shape[1]
+    nz, count, nvec = out_ref.shape[:3]
+    nall = nz * nvec
+    own_at = list_ref.shape[1] - 1 - nz
     copies = []
     for n, (src, dst) in enumerate(
         ((co_l, co_ref), (co_m, co_ref), (co_r, co_ref), (wx_l, wx_ref), (wx_m, wx_ref), (wx_r, wx_ref))
@@ -184,31 +203,35 @@
         c.wait()
 
     def target(t, carry):
-        own = co_ref[list_ref[t, 29]]
+        own = jnp.transpose(co_ref[list_ref[t, own_at]])
         for c in range(3):
-            tgt_ref[c] = jnp.broadcast_to(own[c : c + 1], (128, 128)).T
-
-        def pair(k, acc):
-            his, los, ws = [], [], []
-            for s in range(2):
-                m = list_ref[t, 2 * k + s]
-                co = co_ref[m]
-                d0 = tgt_ref[0] - co[0:1]
-                d1 = tgt_ref[1] - co[1:2]
-                d2 = tgt_ref[2] - co[2:3]
-                kern = lax.rsqrt(d0 * d0 + d1 * d1 + (d2 * d2 + SOFT_SQ))
-                hi, lo = split(kern)
-                his.append(hi)
-                los.append(lo)
-                whi, wlo = split(wx_ref[m])
-                ws.append(jnp.concatenate([whi, wlo], axis=0))
-            rhs = jnp.concatenate(
-                [jnp.concatenate(his, axis=1), jnp.concatenate(los, axis=1)], axis=0
-            )
-            return acc + dot(jnp.concatenate(ws, axis=1), rhs, NT)
-
-        acc = lax.fori_loop(0, list_ref[t, 28], pair, jnp.zeros((2 * nvec, 256), F32))
-        out_ref[t] = acc[:nvec, :128] + acc[nvec:, :128] + acc[:nvec, 128:]
+            tgt_ref[c] = jnp.broadcast_to(own[:, c : c + 1], (128, 128))
+
+        def step(k, acc):
+            for g in range(NEAR_STEP):
+                his, los, ws = [], [], []
+                for s in range(2):
+                    m = list_ref[t, 2 * (k * NEAR_STEP + g) + s]
+                    co = co_ref[m]
+                    d0 = tgt_ref[0] - co[0:1]
+                    d1 = tgt_ref[1] - co[1:2]
+                    d2 = tgt_ref[2] - co[2:3]
+                    kern = lax.rsqrt(d0 * d0 + d1 * d1 + (d2 * d2 + SOFT_SQ))
+                    hi, lo = split(kern)
+                    his.append(hi)
+                    los.append(lo)
+                    whi, wlo = split(wx_ref[m])
+                    ws.append(jnp.concatenate([whi, wlo], axis=0))
+                rhs = jnp.concatenate(
+                    [jnp.concatenate(his, axis=1), jnp.concatenate(los, axis=1)], axis=0
+                )
+                acc = acc + dot(jnp.concatenate(ws, axis=1), rhs, NT)
+            return acc
+
+        acc = lax.fori_loop(0, list_ref[t, own_at - 1], step, jnp.zeros((2 * nall, 256), F32))
+        x = acc[:nall, :128] + acc[nall:, :128] + acc[:nall, 128:]
+        for k in range(nz):
+            out_ref[list_ref[t, own_at + 1 + k], t] = x[k * nvec : (k + 1) * nvec]
         return carry
 
     lax.fori_loop(0, count, target, 0)
@@ -236,7 +259,11 @@
 
     leaf_x = vectors.reshape(nvec, nleaf, width).transpose(1, 0, 2)
     leaf_w = (weights * (1.0 / (4.0 * math.pi))).reshape(nleaf, 1, width)
-    wx = lax.all_gather(leaf_x * leaf_w, "vec", axis=1, tiled=True)
+    piece = leaf_x * leaf_w
+    pieces = [piece] + [
+        lax.ppermute(piece, "vec", [(i, (i + k) % nz) for i in range(nz)]) for k in range(1, nz)
+    ]
+    wx = jnp.concatenate(pieces, axis=1)
     co = jnp.pad(coords.reshape(3, nleaf, width).transpose(1, 0, 2), ((0, 0), (0, 5), (0, 0)))
     co_l, co_r = shift_both(co, "leaf")
 
@@ -252,17 +279,8 @@
     c_l, c_r = shift_both(coeff, "leaf")
     wx_l, wx_r = shift_both(wx, "leaf")
 
-    per = 4
     rows = -(-(nleaf + npar) // 16) * 16
-    idx = jnp.concatenate(
-        [
-            jnp.where(far_leaf >= 0, far_leaf - first, -1),
-            jnp.where(far_parent >= 0, far_parent - first_par + 3 * nleaf, -1),
-            jnp.full((rows - nleaf - npar, noff), -1, jnp.int32),
-        ],
-        axis=0,
-    )
-    idx = idx.reshape(rows, noff // per, per).transpose(1, 0, 2)
+    padded = -(-noff // FAR_STEP) * FAR_STEP
     depth = 256
     cols = nvec * rank
     far_out = pl.pallas_call(
@@ -272,18 +290,21 @@
             pltpu.VMEM((cols // 128, depth, 128), F32),
             pltpu.VMEM((depth, 2 * cols), BF16),
             pltpu.VMEM((cols // 128, nleaf, 128), F32),
+            pltpu.VMEM((-(-noff // 128), rows, 128), jnp.int32),
+            pltpu.VMEM((padded * rank, 128), F32),
         ],
         compiler_params=params,
         name="far",
         cost_estimate=pl.CostEstimate(flops=10**10, bytes_accessed=10**8, transcendentals=0),
-    )(c_l, coeff, c_r, transfer, coupling, idx, basis)
+    )(c_l, coeff, c_r, transfer, coupling.transpose(1, 2, 0), far_leaf, far_parent, basis)
 
     mine = lax.dynamic_slice_in_dim(near_leaf, vec * count, count, axis=0)
     live = mine >= 0
     at = jnp.arange(slots)
     place = jnp.sum(live[:, None, :] & (at[None, None, :] < at[None, :, None]), axis=2)
     empty = 3 * nleaf
-    j = jnp.arange(28)
+    group = 2 * NEAR_STEP
+    j = jnp.arange(-(-slots // group) * group)
     lists = empty + jnp.sum(
         jnp.where(
             live[:, None, :] & (place[:, None, :] == j[None, :, None]),
@@ -292,13 +313,16 @@
         ),
         axis=2,
     )
-    pairs = (jnp.sum(live, axis=1) + 1) // 2
+    steps = (jnp.sum(live, axis=1) + group - 1) // group
     own = nleaf + vec * count + jnp.arange(count)
-    lists = jnp.concatenate([lists, pairs[:, None], own[:, None]], axis=1).astype(jnp.int32)
+    lists = jnp.concatenate(
+        [lists, steps[:, None], own[:, None], jnp.broadcast_to((vec - jnp.arange(nz)) % nz, (count, nz))],
+        axis=1,
+    ).astype(jnp.int32)
     anywhere = pl.BlockSpec(memory_space=pl.ANY)
     near = pl.pallas_call(
         near_kernel,
-        out_shape=jax.ShapeDtypeStruct((count, nall, width), F32),
+        out_shape=jax.ShapeDtypeStruct((nz, count, nvec, width), F32),
         in_specs=[pl.BlockSpec(memory_space=pltpu.SMEM)] + [anywhere] * 6,
         scratch_shapes=[
             pltpu.VMEM((3 * nleaf + 1, 8, width), F32),
@@ -310,7 +334,8 @@
         name="near",
         cost_estimate=pl.CostEstimate(flops=10**10, bytes_accessed=10**8, transcendentals=0),
     )(lists, co_l, co, co_r, wx_l, wx, wx_r)
-    near = lax.all_to_all(near, "vec", split_axis=1, concat_axis=0, tiled=True)
+    near = lax.all_to_all(near, "vec", split_axis=0, concat_axis=0, tiled=True)
+    near = near.reshape(nleaf, nvec, width)
     return far_out + near.transpose(1, 0, 2).reshape(nvec, nleaf * width)
 
 

time: 158 us -> 101 us (0.64)
  Pallas kernels: 89.2 us -> 60.2 us
  local copies, waits for them, and re-layouts: 25.3 us -> 3.84 us
  blocking collectives: 15.1 us -> 0 us
  waiting for transfers between devices: 0.02 us -> 5.79 us
  starting transfers between devices: 23.2 us -> 25.4 us
    pallas_call x1, Pallas kernels: 42.3 us -> 23.5 us  [body(): pl.pallas_call(near_kernel, out_shape=jax.ShapeDtypeStruct((nz, count, nv...]
    all_gather x1 -> x0, blocking collectives: 15.1 us -> none  [body(): wx = lax.all_gather(leaf_x * leaf_w, 'vec', axis=1, tiled=True)]
    unnamed x15 -> x12, local copies, waits for them, and re-layouts: 17.5 us -> 2.51 us
    pallas_call x1, Pallas kernels: 44.4 us -> 34.1 us  [body(): pl.pallas_call(far_kernel, out_shape=jax.ShapeDtypeStruct((nvec, nleaf *...]
    ppermute x0 -> x3, starting transfers between devices: none -> 5.56 us  [body(): lax.ppermute(piece, 'vec', [(i, (i + k) % nz) for i in range(nz)])]
    ppermute x3, waiting for transfers between devices: 0.01 us -> 4.4 us  [shift_both(): from_right = lax.ppermute(x, axis, [(i + 1, i) for i in range(ends)])]
    reshape x2 -> x0, local copies, waits for them, and re-layouts: 3.06 us -> none  [body(): idx = idx.reshape(rows, noff // per, per).transpose(1, 0, 2)]
    ppermute x3, starting transfers between devices: 12.3 us -> 10.1 us  [shift_both(): from_left = lax.ppermute(x, axis, [(i, i + 1) for i in range(ends)])]
  transfers between devices with their start and end apart: 7 -> 10, of which waited for: 0 -> 2; matrix products, arithmetic and copies ran while one was open for 13% -> 3% of each run, Pallas kernels for 57% -> 60%
where the time goes in v2:
time: 101 us; the launch traced here: 99.7 us
  Pallas kernels  60.2 us (60%)
  starting transfers between devices  25.4 us (25%)
  waiting for transfers between devices  5.79 us (6%)
  other arithmetic  4.25 us (4%)
  local copies, waits for them, and re-layouts  3.84 us (4%)
    pallas_call x1, Pallas kernels, body(): pl.pallas_call(far_kernel, out_shape=jax.ShapeDtypeStruct((nvec, nleaf *...  34.1 us
    pallas_call x1, Pallas kernels, body(): pl.pallas_call(near_kernel, out_shape=jax.ShapeDtypeStruct((nz, count, nv...  23.5 us
    ppermute x3, starting transfers between devices, shift_both(): from_left = lax.ppermute(x, axis, [(i, i + 1) for i in range(ends)])  10.1 us
    ppermute x3, starting transfers between devices, shift_both(): from_right = lax.ppermute(x, axis, [(i + 1, i) for i in range(ends)])  6.41 us
    ppermute x3, starting transfers between devices, body(): lax.ppermute(piece, 'vec', [(i, (i + k) % nz) for i in range(nz)])  5.56 us
    ppermute x3, waiting for transfers between devices, shift_both(): from_right = lax.ppermute(x, axis, [(i + 1, i) for i in range(ends)])  4.4 us
    all_to_all x1, starting transfers between devices, body(): near = lax.all_to_all(near, 'vec', split_axis=0, concat_axis=0, tiled=True)  3.34 us
    pallas_call x1, Pallas kernels, body(): pl.pallas_call(up_kernel, out_shape=jax.ShapeDtypeStruct((nleaf, nvec, ra...  2.53 us
  transfers between devices with their start and end apart: 10, of which 2 were waited for; matrix products, arithmetic and copies ran while one was open for 3% of the time, Pallas kernels for 60%

profile of v2, /device:TPU:1, one launch (start us, length us, event | category | flops | bytes accessed | tf_op | source)
XLA Modules:
  0.0 99.7 jit_solution(13422770855981373554)
XLA Ops:
  0.0 0.8 multiply_bitcast_fusion
  0.8 0.9 broadcast_multiply_fusion
  1.7 2.2 %collective-permute-start.4 = (f32[64,4,128]{2,1,0:T(4,128)S(1)}, f32[64,4,128]{2,1,0:T(4,128)S(1)}, u32[]{:S(2)}, u32[]{:S(2)}) collective-permute-start(f32[64,4,128]{2,1,0:T(4,128)S(1)} %broadcast_multiply_fusion), channel_id=1, source_target_pairs={{0,1},{1,2},{2,3},{3,0},{4,5},{5,6},{6,7},{7,4},{8,9},{9,10},{10,1... | collective-permute-start | bytes 393224 | tf_op jit(solution)/shard_map/ppermute | solution.py:264
  3.9 2.3 %collective-permute-start.5 = (f32[64,4,128]{2,1,0:T(4,128)S(1)}, f32[64,4,128]{2,1,0:T(4,128)S(1)}, u32[]{:S(2)}, u32[]{:S(2)}) collective-permute-start(f32[64,4,128]{2,1,0:T(4,128)S(1)} %broadcast_multiply_fusion), channel_id=1, source_target_pairs={{0,2},{1,3},{2,0},{3,1},{4,6},{5,7},{6,4},{7,5},{8,10},{9,11},{10,... | collective-permute-start | bytes 393224 | tf_op jit(solution)/shard_map/ppermute | solution.py:264
  6.2 1.1 %collective-permute-start.6 = (f32[64,4,128]{2,1,0:T(4,128)S(1)}, f32[64,4,128]{2,1,0:T(4,128)S(1)}, u32[]{:S(2)}, u32[]{:S(2)}) collective-permute-start(f32[64,4,128]{2,1,0:T(4,128)S(1)} %broadcast_multiply_fusion), channel_id=1, source_target_pairs={{0,3},{1,0},{2,1},{3,2},{4,7},{5,4},{6,5},{7,6},{8,11},{9,8},{10,9... | collective-permute-start | bytes 393224 | tf_op jit(solution)/shard_map/ppermute | solution.py:264
  7.3 0.9 pad.4.co_m
  8.2 4.5 %collective-permute-start.2 = (f32[64,8,128]{2,1,0:T(8,128)S(1)}, f32[64,8,128]{2,1,0:T(8,128)S(1)}, u32[]{:S(2)}, u32[]{:S(2)}) collective-permute-start(f32[64,8,128]{2,1,0:T(8,128)S(1)} %pad.4.co_m), channel_id=1, source_target_pairs={{0,4},{4,8},{8,12},{1,5},{5,9},{9,13},{2,6},{6,10},{10,14},{3,7},{... | collective-permute-start | bytes 786440 | tf_op jit(solution)/shard_map/ppermute | solution.py:242
  12.7 1.9 %collective-permute-start.3 = (f32[64,8,128]{2,1,0:T(8,128)S(1)}, f32[64,8,128]{2,1,0:T(8,128)S(1)}, u32[]{:S(2)}, u32[]{:S(2)}) collective-permute-start(f32[64,8,128]{2,1,0:T(8,128)S(1)} %pad.4.co_m), channel_id=1, source_target_pairs={{4,0},{8,4},{12,8},{5,1},{9,5},{13,9},{6,2},{10,6},{14,10},{7,3},{... | collective-permute-start | bytes 786440 | tf_op jit(solution)/shard_map/ppermute | solution.py:243
  14.7 0.8 convert_reduce_fusion.1
  15.7 1.6 %copy-done = f32[64,64,128]{2,1,0:T(8,128)S(1)} copy-done((f32[64,64,128]{2,1,0:T(8,128)S(1)}, f32[64,64,128]{2,1,0:T(8,128)}, u32[]{:S(2)}) %copy-start) | copy-done | bytes 2097176
  17.3 0.9 copy-done.2
  18.2 2.5 %up.1 = f32[64,4,64]{2,1,0:T(4,128)S(1)} custom-call(f32[64,4,128]{2,1,0:T(4,128)S(1)} %bitcast.17, f32[64,64,128]{2,1,0:T(8,128)S(1)} %copy-done), custom_call_target="tpu_custom_call" | custom-call | flops 100000000 | bytes 4000000 | tf_op jit(solution)/shard_map/up/pallas_call | solution.py:271
  20.9 0.6 convert_reduce_fusion
  21.4 0.2 select_reduce_fusion
  21.7 3.6 %collective-permute-start = (f32[64,256]{1,0:T(8,128)S(1)}, f32[64,256]{1,0:T(8,128)S(1)}, u32[]{:S(2)}, u32[]{:S(2)}) collective-permute-start(f32[64,256]{1,0:T(8,128)S(1)} %reshape.97.mid_ref), channel_id=1, source_target_pairs={{0,4},{4,8},{8,12},{1,5},{5,9},{9,13},{2,6},{6,10},{10,14},{3,7},{... | collective-permute-start | bytes 196616 | tf_op jit(solution)/shard_map/ppermute | solution.py:242
  25.5 1.9 %collective-permute-start.7 = (f32[64,16,128]{2,1,0:T(8,128)S(1)}, f32[64,16,128]{2,1,0:T(8,128)S(1)}, u32[]{:S(2)}, u32[]{:S(2)}) collective-permute-start(f32[64,16,128]{2,1,0:T(8,128)S(1)} %pad_maximum_fusion.wx_m), channel_id=1, source_target_pairs={{0,4},{4,8},{8,12},{1,5},{5,9},{9,13},{2,6},{6,10},{10,14},{3,7},{... | collective-permute-start | bytes 1572872 | tf_op jit(solution)/shard_map/ppermute | solution.py:242
  27.4 2.4 %collective-permute-start.8 = (f32[64,16,128]{2,1,0:T(8,128)S(1)}, f32[64,16,128]{2,1,0:T(8,128)S(1)}, u32[]{:S(2)}, u32[]{:S(2)}) collective-permute-start(f32[64,16,128]{2,1,0:T(8,128)S(1)} %pad_maximum_fusion.wx_m), channel_id=1, source_target_pairs={{4,0},{8,4},{12,8},{5,1},{9,5},{13,9},{6,2},{10,6},{14,10},{7,3},{... | collective-permute-start | bytes 1572872 | tf_op jit(solution)/shard_map/ppermute | solution.py:243
  30.1 2.1 %collective-permute-start.1 = (f32[64,256]{1,0:T(8,128)S(1)}, f32[64,256]{1,0:T(8,128)S(1)}, u32[]{:S(2)}, u32[]{:S(2)}) collective-permute-start(f32[64,256]{1,0:T(8,128)S(1)} %reshape.97.mid_ref), channel_id=1, source_target_pairs={{4,0},{8,4},{12,8},{5,1},{9,5},{13,9},{6,2},{10,6},{14,10},{7,3},{... | collective-permute-start | bytes 196616 | tf_op jit(solution)/shard_map/ppermute | solution.py:243
  32.1 1.4 %collective-permute-done.7.wx_l = f32[64,16,128]{2,1,0:T(8,128)S(1)} collective-permute-done((f32[64,16,128]{2,1,0:T(8,128)S(1)}, f32[64,16,128]{2,1,0:T(8,128)S(1)}, u32[]{:S(2)}, u32[]{:S(2)}) %collective-permute-start.7) | collective-permute-done | bytes 524320 | tf_op jit(solution)/shard_map/ppermute | solution.py:242
  33.5 4.4 %collective-permute-done.8.wx_r = f32[64,16,128]{2,1,0:T(8,128)S(1)} collective-permute-done((f32[64,16,128]{2,1,0:T(8,128)S(1)}, f32[64,16,128]{2,1,0:T(8,128)S(1)}, u32[]{:S(2)}, u32[]{:S(2)}) %collective-permute-start.8) | collective-permute-done | bytes 524320 | tf_op jit(solution)/shard_map/ppermute | solution.py:243
  37.9 23.5 %near.1 = f32[4,16,4,128]{3,2,1,0:T(4,128)} custom-call(s32[16,38]{1,0:T(8,128)S(1)} %add_add_fusion.list_ref, f32[64,8,128]{2,1,0:T(8,128)S(1)} %collective-permute-done.2.co_l, f32[64,8,128]{2,1,0:T(8,128)S(1)} %pad.4.co_m, f32[64,8,128]{2,1,0:T(8,128)S(1)} %collective-permute-done.3.co_r, f32[64,16,128]{2,1,0:T(8,128)S(1)} %collective-permute-done.7.wx_l, ...), custom_call_target="tpu_custom_call" | custom-call | flops 10000000000 | bytes 100000000 | tf_op jit(solution)/shard_map/near/pallas_call | solution.py:323
  61.4 3.3 %all-to-all-start = ((f32[4,16,4,128]{3,2,1,0:T(4,128)}), f32[4,16,4,128]{3,2,1,0:T(4,128)S(1)}, u32[]{:S(2)}, u32[]{:S(2)}) async-start(f32[4,16,4,128]{3,2,1,0:T(4,128)} %near.1), calls=%async_computation | async-start | bytes 262144 | tf_op jit(solution)/shard_map/all_to_all | solution.py:337
  64.8 34.1 %far.1 = f32[4,8192]{1,0:T(4,128)S(1)} custom-call(f32[64,256]{1,0:T(8,128)S(1)} %collective-permute-done.left_ref, f32[64,256]{1,0:T(8,128)S(1)} %reshape.97.mid_ref, f32[64,256]{1,0:T(8,128)S(1)} %collective-permute-done.1.right_ref, f32[8,64,64]{2,1,0:T(8,128)S(1)} %copy-done.3, f32[64,64,316]{2,1,0:T(8,128)} %bitcast.20, s32[64,316]{1,0:T(8,128)S(1)} %copy-done.4, ...), custom_call_target="tpu_custom_call" | custom-call | flops 10000000000 | bytes 100000000 | tf_op jit(solution)/shard_map/far/pallas_call | solution.py:286
  99.0 0.7 add.63
  (29 shorter events, 0.7 us)
Async XLA Ops:
  1.7 20.0 %collective-permute-start.4 = (f32[64,4,128]{2,1,0:T(4,128)S(1)}, f32[64,4,128]{2,1,0:T(4,128)S(1)}, u32[]{:S(2)}, u32[]{:S(2)}) collective-permute-start(f32[64,4,128]{2,1,0:T(4,128)S(1)} %broadcast_multiply_fusion), channel_id=1, source_target_pairs={{0,1},{1,2},{2,3},{3,0},{4,5},{5,6},{6,7},{7,4},{8,9},{9,10},{10,1... | collective-permute-start | bytes 393224 | tf_op jit(solution)/shard_map/ppermute | solution.py:264
  3.9 21.4 %collective-permute-start.5 = (f32[64,4,128]{2,1,0:T(4,128)S(1)}, f32[64,4,128]{2,1,0:T(4,128)S(1)}, u32[]{:S(2)}, u32[]{:S(2)}) collective-permute-start(f32[64,4,128]{2,1,0:T(4,128)S(1)} %broadcast_multiply_fusion), channel_id=1, source_target_pairs={{0,2},{1,3},{2,0},{3,1},{4,6},{5,7},{6,4},{7,5},{8,10},{9,11},{10,... | collective-permute-start | bytes 393224 | tf_op jit(solution)/shard_map/ppermute | solution.py:264
  6.2 19.2 %collective-permute-start.6 = (f32[64,4,128]{2,1,0:T(4,128)S(1)}, f32[64,4,128]{2,1,0:T(4,128)S(1)}, u32[]{:S(2)}, u32[]{:S(2)}) collective-permute-start(f32[64,4,128]{2,1,0:T(4,128)S(1)} %broadcast_multiply_fusion), channel_id=1, source_target_pairs={{0,3},{1,0},{2,1},{3,2},{4,7},{5,4},{6,5},{7,6},{8,11},{9,8},{10,9... | collective-permute-start | bytes 393224 | tf_op jit(solution)/shard_map/ppermute | solution.py:264
  8.2 21.9 %collective-permute-start.2 = (f32[64,8,128]{2,1,0:T(8,128)S(1)}, f32[64,8,128]{2,1,0:T(8,128)S(1)}, u32[]{:S(2)}, u32[]{:S(2)}) collective-permute-start(f32[64,8,128]{2,1,0:T(8,128)S(1)} %pad.4.co_m), channel_id=1, source_target_pairs={{0,4},{4,8},{8,12},{1,5},{5,9},{9,13},{2,6},{6,10},{10,14},{3,7},{... | collective-permute-start | bytes 786440 | tf_op jit(solution)/shard_map/ppermute | solution.py:242
  12.7 19.4 %collective-permute-start.3 = (f32[64,8,128]{2,1,0:T(8,128)S(1)}, f32[64,8,128]{2,1,0:T(8,128)S(1)}, u32[]{:S(2)}, u32[]{:S(2)}) collective-permute-start(f32[64,8,128]{2,1,0:T(8,128)S(1)} %pad.4.co_m), channel_id=1, source_target_pairs={{4,0},{8,4},{12,8},{5,1},{9,5},{13,9},{6,2},{10,6},{14,10},{7,3},{... | collective-permute-start | bytes 786440 | tf_op jit(solution)/shard_map/ppermute | solution.py:243
  15.7 1.6 %copy-start = (f32[64,64,128]{2,1,0:T(8,128)S(1)}, f32[64,64,128]{2,1,0:T(8,128)}, u32[]{:S(2)}) copy-start(f32[64,64,128]{2,1,0:T(8,128)} %basis_ref.3) | copy-start | bytes 6291460
  17.3 0.9 copy-start.2
  21.7 43.1 %collective-permute-start = (f32[64,256]{1,0:T(8,128)S(1)}, f32[64,256]{1,0:T(8,128)S(1)}, u32[]{:S(2)}, u32[]{:S(2)}) collective-permute-start(f32[64,256]{1,0:T(8,128)S(1)} %reshape.97.mid_ref), channel_id=1, source_target_pairs={{0,4},{4,8},{8,12},{1,5},{5,9},{9,13},{2,6},{6,10},{10,14},{3,7},{... | collective-permute-start | bytes 196616 | tf_op jit(solution)/shard_map/ppermute | solution.py:242
  25.5 8.0 %collective-permute-start.7 = (f32[64,16,128]{2,1,0:T(8,128)S(1)}, f32[64,16,128]{2,1,0:T(8,128)S(1)}, u32[]{:S(2)}, u32[]{:S(2)}) collective-permute-start(f32[64,16,128]{2,1,0:T(8,128)S(1)} %pad_maximum_fusion.wx_m), channel_id=1, source_target_pairs={{0,4},{4,8},{8,12},{1,5},{5,9},{9,13},{2,6},{6,10},{10,14},{3,7},{... | collective-permute-start | bytes 1572872 | tf_op jit(solution)/shard_map/ppermute | solution.py:242
  27.4 10.5 %collective-permute-start.8 = (f32[64,16,128]{2,1,0:T(8,128)S(1)}, f32[64,16,128]{2,1,0:T(8,128)S(1)}, u32[]{:S(2)}, u32[]{:S(2)}) collective-permute-start(f32[64,16,128]{2,1,0:T(8,128)S(1)} %pad_maximum_fusion.wx_m), channel_id=1, source_target_pairs={{4,0},{8,4},{12,8},{5,1},{9,5},{13,9},{6,2},{10,6},{14,10},{7,3},{... | collective-permute-start | bytes 1572872 | tf_op jit(solution)/shard_map/ppermute | solution.py:243
  30.0 34.7 %copy-start.1 = (f32[64,64,128]{2,1,0:T(8,128)S(1)}, f32[64,64,128]{2,1,0:T(8,128)}, u32[]{:S(2)}) copy-start(f32[64,64,128]{2,1,0:T(8,128)} %basis_ref.3) | copy-start | bytes 6291460
  30.0 34.8 %copy-start.3 = (f32[8,64,64]{2,1,0:T(8,128)S(1)}, f32[8,64,64]{2,1,0:T(8,128)}, u32[]{:S(2)}) copy-start(f32[8,64,64]{2,1,0:T(8,128)} %transfer_ref.1) | copy-start | bytes 393220
  30.0 34.8 %copy-start.4 = (s32[64,316]{1,0:T(8,128)S(1)}, s32[64,316]{1,0:T(8,128)}, u32[]{:S(2)}) copy-start(s32[64,316]{1,0:T(8,128)} %leaf_ref.1) | copy-start | bytes 242692
  30.1 34.8 %copy-start.5 = (s32[8,316]{1,0:T(8,128)S(1)}, s32[8,316]{1,0:T(8,128)}, u32[]{:S(2)}) copy-start(s32[8,316]{1,0:T(8,128)} %parent_ref.1) | copy-start | bytes 30340
  30.1 34.7 %collective-permute-start.1 = (f32[64,256]{1,0:T(8,128)S(1)}, f32[64,256]{1,0:T(8,128)S(1)}, u32[]{:S(2)}, u32[]{:S(2)}) collective-permute-start(f32[64,256]{1,0:T(8,128)S(1)} %reshape.97.mid_ref), channel_id=1, source_target_pairs={{4,0},{8,4},{12,8},{5,1},{9,5},{13,9},{6,2},{10,6},{14,10},{7,3},{... | collective-permute-start | bytes 196616 | tf_op jit(solution)/shard_map/ppermute | solution.py:243
  61.4 37.5 %all-to-all-start = ((f32[4,16,4,128]{3,2,1,0:T(4,128)}), f32[4,16,4,128]{3,2,1,0:T(4,128)S(1)}, u32[]{:S(2)}, u32[]{:S(2)}) async-start(f32[4,16,4,128]{3,2,1,0:T(4,128)} %near.1), calls=%async_computation | async-start | bytes 262144 | tf_op jit(solution)/shard_map/all_to_all | solution.py:337

commit v3 on v2

--- a/solution.py
+++ b/solution.py
@@ -41,9 +41,39 @@
     )
 
 
-def up_kernel(x_ref, basis_ref, out_ref):
+def link_kernel(
+    x_ref, w_ref, co_ref, basis_ref,
+    wx_ref, co_l, co_r, c_l, c_m, c_r,
+    piece, own, send_sem, recv_sem, copy_sem,
+):
     nleaf, nvec, _ = x_ref.shape
     rank = basis_ref.shape[1]
+    nz = wx_ref.shape[0]
+    nl = lax.axis_size("leaf")
+    vec, leaf_at = lax.axis_index("vec"), lax.axis_index("leaf")
+    right, left = lax.rem(leaf_at + 1, nl), lax.rem(leaf_at + nl - 1, nl)
+    peers = [{"vec": lax.rem(vec + k, nz)} for k in range(1, nz)]
+    mesh_id = pl.DeviceIdType.MESH
+
+    barrier = pltpu.get_barrier_semaphore()
+    for who in peers + [{"leaf": right}, {"leaf": left}]:
+        pl.semaphore_signal(barrier, inc=1, device_id=who, device_id_type=mesh_id)
+    piece[...] = x_ref[...] * w_ref[...]
+    pl.semaphore_wait(barrier, nz + 1)
+
+    def send(n, src, dst, who):
+        copy = pltpu.make_async_remote_copy(
+            src_ref=src, dst_ref=dst, send_sem=send_sem.at[n], recv_sem=recv_sem.at[n],
+            device_id=who, device_id_type=mesh_id,
+        )
+        copy.start()
+        return copy
+
+    sent = [send(n, piece, wx_ref.at[vec], who) for n, who in enumerate(peers)]
+    sent.append(send(nz - 1, co_ref, co_l, {"leaf": right}))
+    sent.append(send(nz, co_ref, co_r, {"leaf": left}))
+    keep = pltpu.make_async_copy(piece, wx_ref.at[vec], copy_sem.at[0])
+    keep.start()
 
     def step(leaf, carry):
         x = x_ref[leaf]
@@ -51,10 +81,19 @@
         lhs = jnp.concatenate([xhi, x - xhi], axis=0).astype(BF16)
         bhi, blo = split(basis_ref[leaf])
         r = dot(lhs, jnp.concatenate([bhi, blo], axis=0), NT)
-        out_ref[leaf] = r[:nvec, :rank] + r[nvec:, :rank] + r[:nvec, rank:]
+        c = r[:nvec, :rank] + r[nvec:, :rank] + r[:nvec, rank:]
+        own[pl.ds(leaf, 1), :] = jnp.concatenate([c[v : v + 1] for v in range(nvec)], axis=1)
         return carry
 
     lax.fori_loop(0, nleaf, step, 0, unroll=8)
+    sent.append(send(nz + 1, own, c_l, {"leaf": right}))
+    sent.append(send(nz + 2, own, c_r, {"leaf": left}))
+    keep_c = pltpu.make_async_copy(own, c_m, copy_sem.at[1])
+    keep_c.start()
+    for copy in sent:
+        copy.wait()
+    keep.wait()
+    keep_c.wait()
 
 
 def far_kernel(
@@ -259,30 +298,39 @@
 
     leaf_x = vectors.reshape(nvec, nleaf, width).transpose(1, 0, 2)
     leaf_w = (weights * (1.0 / (4.0 * math.pi))).reshape(nleaf, 1, width)
-    piece = leaf_x * leaf_w
-    pieces = [piece] + [
-        lax.ppermute(piece, "vec", [(i, (i + k) % nz) for i in range(nz)]) for k in range(1, nz)
-    ]
-    wx = jnp.concatenate(pieces, axis=1)
     co = jnp.pad(coords.reshape(3, nleaf, width).transpose(1, 0, 2), ((0, 0), (0, 5), (0, 0)))
-    co_l, co_r = shift_both(co, "leaf")
-
     params = pltpu.CompilerParams(vmem_limit_bytes=VMEM_BYTES)
-    coeff = pl.pallas_call(
-        up_kernel,
-        out_shape=jax.ShapeDtypeStruct((nleaf, nvec, rank), F32),
-        compiler_params=params,
-        name="up",
+    cols = nvec * rank
+    in_vmem = pl.BlockSpec(memory_space=pltpu.VMEM)
+    anywhere = pl.BlockSpec(memory_space=pl.ANY)
+    side = jax.ShapeDtypeStruct((nleaf, cols), F32)
+    co_side = jax.ShapeDtypeStruct(co.shape, F32)
+    wx, co_l, co_r, c_l, coeff, c_r = pl.pallas_call(
+        link_kernel,
+        out_shape=(
+            jax.ShapeDtypeStruct((nz, nleaf, nvec, width), F32), co_side, co_side, side, side, side,
+        ),
+        in_specs=[in_vmem] * 4,
+        out_specs=(anywhere,) * 6,
+        scratch_shapes=[
+            pltpu.VMEM((nleaf, nvec, width), F32),
+            pltpu.VMEM((nleaf, cols), F32),
+            pltpu.SemaphoreType.DMA((nz + 3,)),
+            pltpu.SemaphoreType.DMA((nz + 3,)),
+            pltpu.SemaphoreType.DMA((2,)),
+        ],
+        compiler_params=pltpu.CompilerParams(
+            vmem_limit_bytes=VMEM_BYTES, collective_id=0, has_side_effects=True
+        ),
+        name="link",
         cost_estimate=pl.CostEstimate(flops=10**8, bytes_accessed=4 * 10**6, transcendentals=0),
-    )(leaf_x, basis)
-    coeff = coeff.reshape(nleaf, nvec * rank)
-    c_l, c_r = shift_both(coeff, "leaf")
+    )(leaf_x, leaf_w, co, basis)
+    wx = wx.transpose(1, 0, 2, 3).reshape(nleaf, nz * nvec, width)
     wx_l, wx_r = shift_both(wx, "leaf")
 
     rows = -(-(nleaf + npar) // 16) * 16
     padded = -(-noff // FAR_STEP) * FAR_STEP
     depth = 256
-    cols = nvec * rank
     far_out = pl.pallas_call(
         far_kernel,
         out_shape=jax.ShapeDtypeStruct((nvec, nleaf * width), F32),
@@ -316,10 +364,9 @@
     steps = (jnp.sum(live, axis=1) + group - 1) // group
     own = nleaf + vec * count + jnp.arange(count)
     lists = jnp.concatenate(
-        [lists, steps[:, None], own[:, None], jnp.broadcast_to((vec - jnp.arange(nz)) % nz, (count, nz))],
+        [lists, steps[:, None], own[:, None], jnp.broadcast_to(jnp.arange(nz), (count, nz))],
         axis=1,
     ).astype(jnp.int32)
-    anywhere = pl.BlockSpec(memory_space=pl.ANY)
     near = pl.pallas_call(
         near_kernel,
         out_shape=jax.ShapeDtypeStruct((nz, count, nvec, width), F32),

time: 101 us -> 104 us (1.030)
  starting transfers between devices: 25.4 us -> 13.1 us
  Pallas kernels: 60.2 us -> 71.4 us
  local copies, waits for them, and re-layouts: 3.84 us -> 11.5 us
  waiting for transfers between devices: 5.79 us -> 4.13 us
  other arithmetic: 4.25 us -> 3.17 us
    pallas_call x1, Pallas kernels: 2.53 us -> 14.2 us  [body(): pl.pallas_call(link_kernel, out_shape=(jax.ShapeDtypeStruct((nz, nleaf, n...]
    unnamed x12 -> x36, local copies, waits for them, and re-layouts: 2.51 us -> 10.3 us
    ppermute x3 -> x1, starting transfers between devices: 10.1 us -> 2.57 us  [shift_both(): from_left = lax.ppermute(x, axis, [(i, i + 1) for i in range(ends)])]
    ppermute x3 -> x0, starting transfers between devices: 5.56 us -> none  [body(): lax.ppermute(piece, 'vec', [(i, (i + k) % nz) for i in range(nz)])]
    all_to_all x1, starting transfers between devices: 3.34 us -> 7.01 us  [body(): near = lax.all_to_all(near, 'vec', split_axis=0, concat_axis=0, tiled=True)]
    ppermute x3 -> x1, starting transfers between devices: 6.41 us -> 3.51 us  [shift_both(): from_right = lax.ppermute(x, axis, [(i + 1, i) for i in range(ends)])]
    ppermute x3 -> x1, waiting for transfers between devices: 4.4 us -> 2.94 us  [shift_both(): from_right = lax.ppermute(x, axis, [(i + 1, i) for i in range(ends)])]
  transfers between devices with their start and end apart: 10 -> 3, of which waited for: 2 -> 2; matrix products, arithmetic and copies ran while one was open for 3% -> 2% of each run, Pallas kernels for 60% -> 33%
where the time goes in v3:
time: 104 us; the launch traced here: 103 us
  Pallas kernels  71.4 us (69%)
  starting transfers between devices  13.1 us (13%)
  local copies, waits for them, and re-layouts  11.5 us (11%)
  waiting for transfers between devices  4.13 us (4%)
  other arithmetic  3.17 us (3%)
    pallas_call x1, Pallas kernels, body(): pl.pallas_call(far_kernel, out_shape=jax.ShapeDtypeStruct((nvec, nleaf *...  34.1 us
    pallas_call x1, Pallas kernels, body(): pl.pallas_call(near_kernel, out_shape=jax.ShapeDtypeStruct((nz, count, nv...  23.1 us
    pallas_call x1, Pallas kernels, body(): pl.pallas_call(link_kernel, out_shape=(jax.ShapeDtypeStruct((nz, nleaf, n...  14.2 us
    unnamed x36, local copies, waits for them, and re-layouts  10.3 us
    all_to_all x1, starting transfers between devices, body(): near = lax.all_to_all(near, 'vec', split_axis=0, concat_axis=0, tiled=True)  7.01 us
    ppermute x1, starting transfers between devices, shift_both(): from_right = lax.ppermute(x, axis, [(i + 1, i) for i in range(ends)])  3.51 us
    ppermute x1, waiting for transfers between devices, shift_both(): from_right = lax.ppermute(x, axis, [(i + 1, i) for i in range(ends)])  2.94 us
    ppermute x1, starting transfers between devices, shift_both(): from_left = lax.ppermute(x, axis, [(i, i + 1) for i in range(ends)])  2.57 us
  transfers between devices with their start and end apart: 3, of which 2 were waited for; matrix products, arithmetic and copies ran while one was open for 2% of the time, Pallas kernels for 33%

profile of v3, /device:TPU:1, one launch (start us, length us, event | category | flops | bytes accessed | tf_op | source)
XLA Modules:
  0.0 103.5 jit_solution(2518777078819281300)
XLA Ops:
  0.0 0.8 broadcast_multiply_fusion
  0.8 0.9 pad.4.co_ref.co_m
  1.7 1.6 %copy-done = f32[64,64,128]{2,1,0:T(8,128)S(1)} copy-done((f32[64,64,128]{2,1,0:T(8,128)S(1)}, f32[64,64,128]{2,1,0:T(8,128)}, u32[]{:S(2)}) %copy-start) | copy-done | bytes 2097176
  3.3 0.9 copy-done.2
  4.2 14.2 %link.1 = (f32[4,64,4,128]{3,2,1,0:T(4,128)S(1)}, f32[64,8,128]{2,1,0:T(8,128)S(1)}, f32[64,8,128]{2,1,0:T(8,128)S(1)}, f32[64,256]{1,0:T(8,128)S(1)}, f32[64,256]{1,0:T(8,128)S(1)}, /*index=5*/f32[64,256]{1,0:T(8,128)S(1)}) custom-call(f32[64,4,128]{2,1,0:T(4,128)S(1)} %bitcast.22, f32[64,1,128]{2,1,0:T(1,128)S(1)} %bitcast.21, ...), custom_call_target="tpu_custom_call" | custom-call | flops 100000000 | bytes 4000000 | tf_op jit(solution)/shard_map/link/pallas_call | solution.py:308
  18.5 0.6 copy-done.6
  19.1 3.5 %collective-permute-start.1 = (f32[64,16,128]{2,1,0:T(8,128)S(1)}, f32[64,16,128]{2,1,0:T(8,128)S(1)}, u32[]{:S(2)}, u32[]{:S(2)}) collective-permute-start(f32[64,16,128]{2,1,0:T(8,128)S(1)} %bitcast.17), channel_id=1, source_target_pairs={{4,0},{8,4},{12,8},{5,1},{9,5},{13,9},{6,2},{10,6},{14,10},{7,3},{... | collective-permute-start | bytes 1572872 | tf_op jit(solution)/shard_map/ppermute | solution.py:282
  22.6 2.6 %collective-permute-start = (f32[64,16,128]{2,1,0:T(8,128)S(1)}, f32[64,16,128]{2,1,0:T(8,128)S(1)}, u32[]{:S(2)}, u32[]{:S(2)}) collective-permute-start(f32[64,16,128]{2,1,0:T(8,128)S(1)} %bitcast.18), channel_id=1, source_target_pairs={{0,4},{4,8},{8,12},{1,5},{5,9},{9,13},{2,6},{6,10},{10,14},{3,7},{... | collective-permute-start | bytes 1572872 | tf_op jit(solution)/shard_map/ppermute | solution.py:281
  25.2 0.8 convert_reduce_fusion.1
  26.2 0.6 convert_reduce_fusion
  27.2 2.9 %collective-permute-done.1.wx_r = f32[64,16,128]{2,1,0:T(8,128)S(1)} collective-permute-done((f32[64,16,128]{2,1,0:T(8,128)S(1)}, f32[64,16,128]{2,1,0:T(8,128)S(1)}, u32[]{:S(2)}, u32[]{:S(2)}) %collective-permute-start.1) | collective-permute-done | bytes 524320 | tf_op jit(solution)/shard_map/ppermute | solution.py:282
  30.1 1.2 %collective-permute-done.wx_l = f32[64,16,128]{2,1,0:T(8,128)S(1)} collective-permute-done((f32[64,16,128]{2,1,0:T(8,128)S(1)}, f32[64,16,128]{2,1,0:T(8,128)S(1)}, u32[]{:S(2)}, u32[]{:S(2)}) %collective-permute-start) | collective-permute-done | bytes 524320 | tf_op jit(solution)/shard_map/ppermute | solution.py:281
  31.3 0.8 copy-done.3
  32.1 1.0 %copy-done.4 = f32[64,16,128]{2,1,0:T(8,128)S(1)} copy-done((f32[64,16,128]{2,1,0:T(8,128)S(1)}, f32[64,16,128]{2,1,0:T(8,128)}, u32[]{:S(2)}) %copy-start.4) | copy-done | bytes 524312
  33.1 0.9 copy-done.7
  34.1 0.9 copy-done.9
  35.0 23.1 %near.1 = f32[4,16,4,128]{3,2,1,0:T(4,128)} custom-call(s32[16,38]{1,0:T(8,128)S(1)} %pad_add_fusion.list_ref, f32[64,8,128]{2,1,0:T(8,128)S(1)} %copy-done.7, f32[64,8,128]{2,1,0:T(8,128)S(1)} %pad.4.co_ref.co_m, f32[64,8,128]{2,1,0:T(8,128)S(1)} %copy-done.9, f32[64,16,128]{2,1,0:T(8,128)S(1)} %copy-done.4, f32[64,16,128]{2,1,0:T(8,128)S(1)} %bitcast.19, ...), custom_call_target="tpu_custom_call" | custom-call | flops 10000000000 | bytes 100000000 | tf_op jit(solution)/shard_map/near/pallas_call | solution.py:370
  58.2 7.0 %all-to-all-start = ((f32[4,16,4,128]{3,2,1,0:T(4,128)}), f32[4,16,4,128]{3,2,1,0:T(4,128)S(1)}, u32[]{:S(2)}, u32[]{:S(2)}) async-start(f32[4,16,4,128]{3,2,1,0:T(4,128)} %near.1), calls=%async_computation | async-start | bytes 262144 | tf_op jit(solution)/shard_map/all_to_all | solution.py:384
  65.2 0.9 copy-done.5
  66.1 0.8 copy-done.12
  67.0 0.8 copy-done.14
  67.8 0.8 copy-done.16
  68.7 34.1 %far.1 = f32[4,8192]{1,0:T(4,128)S(1)} custom-call(f32[64,256]{1,0:T(8,128)S(1)} %copy-done.12, f32[64,256]{1,0:T(8,128)S(1)} %copy-done.14, f32[64,256]{1,0:T(8,128)S(1)} %copy-done.16, f32[8,64,64]{2,1,0:T(8,128)S(1)} %copy-done.5, f32[64,64,316]{2,1,0:T(8,128)} %bitcast.25, s32[64,316]{1,0:T(8,128)S(1)} %copy-done.10, s32[8,316]{1,0:T(8,128)S(1)} %copy-done.17, ...), custom_call_target="tpu_custom_call" | custom-call | flops 10000000000 | bytes 100000000 | tf_op jit(solution)/shard_map/far/pallas_call | solution.py:334
  102.8 0.7 add.56
  (36 shorter events, 0.7 us)
Async XLA Ops:
  1.7 1.6 %copy-start = (f32[64,64,128]{2,1,0:T(8,128)S(1)}, f32[64,64,128]{2,1,0:T(8,128)}, u32[]{:S(2)}) copy-start(f32[64,64,128]{2,1,0:T(8,128)} %basis_ref.3) | copy-start | bytes 6291460
  3.3 0.9 copy-start.2
  18.4 0.7 copy-start.6
  18.4 4.2 %copy-start.8 = (f32[64,8,128]{2,1,0:T(8,128)}, f32[64,8,128]{2,1,0:T(8,128)S(1)}, u32[]{:S(2)}) copy-start(f32[64,8,128]{2,1,0:T(8,128)S(1)} %get-tuple-element.15.co_r) | copy-start | bytes 786436
  18.4 6.8 %copy-start.11 = (f32[64,256]{1,0:T(8,128)}, f32[64,256]{1,0:T(8,128)S(1)}, u32[]{:S(2)}) copy-start(f32[64,256]{1,0:T(8,128)S(1)} %get-tuple-element.11.left_ref) | copy-start | bytes 196612
  18.4 6.8 %copy-start.13 = (f32[64,256]{1,0:T(8,128)}, f32[64,256]{1,0:T(8,128)S(1)}, u32[]{:S(2)}) copy-start(f32[64,256]{1,0:T(8,128)S(1)} %get-tuple-element.12.mid_ref) | copy-start | bytes 196612
  18.4 6.8 %copy-start.15 = (f32[64,256]{1,0:T(8,128)}, f32[64,256]{1,0:T(8,128)S(1)}, u32[]{:S(2)}) copy-start(f32[64,256]{1,0:T(8,128)S(1)} %get-tuple-element.13.right_ref) | copy-start | bytes 196612
  19.1 11.0 %collective-permute-start.1 = (f32[64,16,128]{2,1,0:T(8,128)S(1)}, f32[64,16,128]{2,1,0:T(8,128)S(1)}, u32[]{:S(2)}, u32[]{:S(2)}) collective-permute-start(f32[64,16,128]{2,1,0:T(8,128)S(1)} %bitcast.17), channel_id=1, source_target_pairs={{4,0},{8,4},{12,8},{5,1},{9,5},{13,9},{6,2},{10,6},{14,10},{7,3},{... | collective-permute-start | bytes 1572872 | tf_op jit(solution)/shard_map/ppermute | solution.py:282
  22.6 8.7 %collective-permute-start = (f32[64,16,128]{2,1,0:T(8,128)S(1)}, f32[64,16,128]{2,1,0:T(8,128)S(1)}, u32[]{:S(2)}, u32[]{:S(2)}) collective-permute-start(f32[64,16,128]{2,1,0:T(8,128)S(1)} %bitcast.18), channel_id=1, source_target_pairs={{0,4},{4,8},{8,12},{1,5},{5,9},{9,13},{2,6},{6,10},{10,14},{3,7},{... | collective-permute-start | bytes 1572872 | tf_op jit(solution)/shard_map/ppermute | solution.py:281
  31.3 0.8 copy-start.3
  32.1 1.0 %copy-start.4 = (f32[64,16,128]{2,1,0:T(8,128)S(1)}, f32[64,16,128]{2,1,0:T(8,128)}, u32[]{:S(2)}) copy-start(f32[64,16,128]{2,1,0:T(8,128)} %copy-done.3) | copy-start | bytes 1572868
  33.1 0.9 copy-start.7
  34.1 0.9 copy-start.9
  35.0 30.1 %copy-start.1 = (f32[64,64,128]{2,1,0:T(8,128)S(1)}, f32[64,64,128]{2,1,0:T(8,128)}, u32[]{:S(2)}) copy-start(f32[64,64,128]{2,1,0:T(8,128)} %basis_ref.3) | copy-start | bytes 6291460
  35.0 30.1 %copy-start.10 = (s32[64,316]{1,0:T(8,128)S(1)}, s32[64,316]{1,0:T(8,128)}, u32[]{:S(2)}) copy-start(s32[64,316]{1,0:T(8,128)} %leaf_ref.1) | copy-start | bytes 242692
  35.0 30.1 %copy-start.17 = (s32[8,316]{1,0:T(8,128)S(1)}, s32[8,316]{1,0:T(8,128)}, u32[]{:S(2)}) copy-start(s32[8,316]{1,0:T(8,128)} %parent_ref.1) | copy-start | bytes 30340
  58.2 44.6 %all-to-all-start = ((f32[4,16,4,128]{3,2,1,0:T(4,128)}), f32[4,16,4,128]{3,2,1,0:T(4,128)S(1)}, u32[]{:S(2)}, u32[]{:S(2)}) async-start(f32[4,16,4,128]{3,2,1,0:T(4,128)} %near.1), calls=%async_computation | async-start | bytes 262144 | tf_op jit(solution)/shard_map/all_to_all | solution.py:384
  65.2 1.0 copy-start.5
  66.1 0.8 copy-start.12
  67.0 0.8 copy-start.14
  67.8 0.8 copy-start.16

commit v4 on v2

--- a/solution.py
+++ b/solution.py
@@ -11,8 +11,8 @@
 SOFT_SQ = 0.0001
 F32 = jnp.float32
 BF16 = jnp.bfloat16
-FAR_STEP = 32
-NEAR_STEP = 4
+FAR_STEP = 64
+NEAR_STEP = 7
 VMEM_BYTES = 48 * 1024 * 1024
 NT = (((1,), (1,)), ((), ()))
 NN = (((1,), (0,)), ((), ()))

time: 101 us -> 98.6 us (0.976); the launches traced: 99.7 us -> 98.3 us
  Pallas kernels: 60.2 us -> 58.5 us
    pallas_call x1, Pallas kernels: 34.1 us -> 32.5 us  [body(): pl.pallas_call(far_kernel, out_shape=jax.ShapeDtypeStruct((nvec, nleaf *...]
where the time goes in v4:
time: 98.6 us; the launch traced here: 98.3 us
  Pallas kernels  58.5 us (59%)
  starting transfers between devices  25.6 us (26%)
  waiting for transfers between devices  5.79 us (6%)
  other arithmetic  4.28 us (4%)
  local copies, waits for them, and re-layouts  3.94 us (4%)
    pallas_call x1, Pallas kernels, body(): pl.pallas_call(far_kernel, out_shape=jax.ShapeDtypeStruct((nvec, nleaf *...  32.5 us
    pallas_call x1, Pallas kernels, body(): pl.pallas_call(near_kernel, out_shape=jax.ShapeDtypeStruct((nz, count, nv...  23.5 us
    ppermute x3, starting transfers between devices, shift_both(): from_left = lax.ppermute(x, axis, [(i, i + 1) for i in range(ends)])  10.1 us
    ppermute x3, starting transfers between devices, shift_both(): from_right = lax.ppermute(x, axis, [(i + 1, i) for i in range(ends)])  6.41 us
    ppermute x3, starting transfers between devices, body(): lax.ppermute(piece, 'vec', [(i, (i + k) % nz) for i in range(nz)])  5.56 us
    ppermute x3, waiting for transfers between devices, shift_both(): from_right = lax.ppermute(x, axis, [(i + 1, i) for i in range(ends)])  4.4 us
    all_to_all x1, starting transfers between devices, body(): near = lax.all_to_all(near, 'vec', split_axis=0, concat_axis=0, tiled=True)  3.52 us
    pallas_call x1, Pallas kernels, body(): pl.pallas_call(up_kernel, out_shape=jax.ShapeDtypeStruct((nleaf, nvec, ra...  2.53 us
  transfers between devices with their start and end apart: 10, of which 2 were waited for; matrix products, arithmetic and copies ran while one was open for 3% of the time, Pallas kernels for 60%

profile of v4, /device:TPU:1, one launch (start us, length us, event | category | flops | bytes accessed | tf_op | source)
XLA Modules:
  0.0 98.3 jit_solution(7039161216134509259)
XLA Ops:
  0.0 0.8 multiply_bitcast_fusion
  0.8 0.9 broadcast_multiply_fusion
  1.7 2.2 %collective-permute-start.4 = (f32[64,4,128]{2,1,0:T(4,128)S(1)}, f32[64,4,128]{2,1,0:T(4,128)S(1)}, u32[]{:S(2)}, u32[]{:S(2)}) collective-permute-start(f32[64,4,128]{2,1,0:T(4,128)S(1)} %broadcast_multiply_fusion), channel_id=1, source_target_pairs={{0,1},{1,2},{2,3},{3,0},{4,5},{5,6},{6,7},{7,4},{8,9},{9,10},{10,1... | collective-permute-start | bytes 393224 | tf_op jit(solution)/shard_map/ppermute | solution.py:264
  3.9 2.3 %collective-permute-start.5 = (f32[64,4,128]{2,1,0:T(4,128)S(1)}, f32[64,4,128]{2,1,0:T(4,128)S(1)}, u32[]{:S(2)}, u32[]{:S(2)}) collective-permute-start(f32[64,4,128]{2,1,0:T(4,128)S(1)} %broadcast_multiply_fusion), channel_id=1, source_target_pairs={{0,2},{1,3},{2,0},{3,1},{4,6},{5,7},{6,4},{7,5},{8,10},{9,11},{10,... | collective-permute-start | bytes 393224 | tf_op jit(solution)/shard_map/ppermute | solution.py:264
  6.2 1.1 %collective-permute-start.6 = (f32[64,4,128]{2,1,0:T(4,128)S(1)}, f32[64,4,128]{2,1,0:T(4,128)S(1)}, u32[]{:S(2)}, u32[]{:S(2)}) collective-permute-start(f32[64,4,128]{2,1,0:T(4,128)S(1)} %broadcast_multiply_fusion), channel_id=1, source_target_pairs={{0,3},{1,0},{2,1},{3,2},{4,7},{5,4},{6,5},{7,6},{8,11},{9,8},{10,9... | collective-permute-start | bytes 393224 | tf_op jit(solution)/shard_map/ppermute | solution.py:264
  7.3 0.9 pad.4.co_m
  8.2 4.5 %collective-permute-start.2 = (f32[64,8,128]{2,1,0:T(8,128)S(1)}, f32[64,8,128]{2,1,0:T(8,128)S(1)}, u32[]{:S(2)}, u32[]{:S(2)}) collective-permute-start(f32[64,8,128]{2,1,0:T(8,128)S(1)} %pad.4.co_m), channel_id=1, source_target_pairs={{0,4},{4,8},{8,12},{1,5},{5,9},{9,13},{2,6},{6,10},{10,14},{3,7},{... | collective-permute-start | bytes 786440 | tf_op jit(solution)/shard_map/ppermute | solution.py:242
  12.7 1.9 %collective-permute-start.3 = (f32[64,8,128]{2,1,0:T(8,128)S(1)}, f32[64,8,128]{2,1,0:T(8,128)S(1)}, u32[]{:S(2)}, u32[]{:S(2)}) collective-permute-start(f32[64,8,128]{2,1,0:T(8,128)S(1)} %pad.4.co_m), channel_id=1, source_target_pairs={{4,0},{8,4},{12,8},{5,1},{9,5},{13,9},{6,2},{10,6},{14,10},{7,3},{... | collective-permute-start | bytes 786440 | tf_op jit(solution)/shard_map/ppermute | solution.py:243
  14.7 0.8 convert_reduce_fusion.1
  15.8 1.6 %copy-done = f32[64,64,128]{2,1,0:T(8,128)S(1)} copy-done((f32[64,64,128]{2,1,0:T(8,128)S(1)}, f32[64,64,128]{2,1,0:T(8,128)}, u32[]{:S(2)}) %copy-start) | copy-done | bytes 2097176
  17.4 0.9 copy-done.2
  18.3 2.5 %up.1 = f32[64,4,64]{2,1,0:T(4,128)S(1)} custom-call(f32[64,4,128]{2,1,0:T(4,128)S(1)} %bitcast.19, f32[64,64,128]{2,1,0:T(8,128)S(1)} %copy-done), custom_call_target="tpu_custom_call" | custom-call | flops 100000000 | bytes 4000000 | tf_op jit(solution)/shard_map/up/pallas_call | solution.py:271
  21.0 0.6 convert_reduce_fusion
  21.5 0.2 select_reduce_fusion
  21.8 3.6 %collective-permute-start = (f32[64,256]{1,0:T(8,128)S(1)}, f32[64,256]{1,0:T(8,128)S(1)}, u32[]{:S(2)}, u32[]{:S(2)}) collective-permute-start(f32[64,256]{1,0:T(8,128)S(1)} %reshape.86.mid_ref), channel_id=1, source_target_pairs={{0,4},{4,8},{8,12},{1,5},{5,9},{9,13},{2,6},{6,10},{10,14},{3,7},{... | collective-permute-start | bytes 196616 | tf_op jit(solution)/shard_map/ppermute | solution.py:242
  25.6 1.9 %collective-permute-start.7 = (f32[64,16,128]{2,1,0:T(8,128)S(1)}, f32[64,16,128]{2,1,0:T(8,128)S(1)}, u32[]{:S(2)}, u32[]{:S(2)}) collective-permute-start(f32[64,16,128]{2,1,0:T(8,128)S(1)} %pad_maximum_fusion.wx_m), channel_id=1, source_target_pairs={{0,4},{4,8},{8,12},{1,5},{5,9},{9,13},{2,6},{6,10},{10,14},{3,7},{... | collective-permute-start | bytes 1572872 | tf_op jit(solution)/shard_map/ppermute | solution.py:242
  27.5 2.4 %collective-permute-start.8 = (f32[64,16,128]{2,1,0:T(8,128)S(1)}, f32[64,16,128]{2,1,0:T(8,128)S(1)}, u32[]{:S(2)}, u32[]{:S(2)}) collective-permute-start(f32[64,16,128]{2,1,0:T(8,128)S(1)} %pad_maximum_fusion.wx_m), channel_id=1, source_target_pairs={{4,0},{8,4},{12,8},{5,1},{9,5},{13,9},{6,2},{10,6},{14,10},{7,3},{... | collective-permute-start | bytes 1572872 | tf_op jit(solution)/shard_map/ppermute | solution.py:243
  30.2 2.1 %collective-permute-start.1 = (f32[64,256]{1,0:T(8,128)S(1)}, f32[64,256]{1,0:T(8,128)S(1)}, u32[]{:S(2)}, u32[]{:S(2)}) collective-permute-start(f32[64,256]{1,0:T(8,128)S(1)} %reshape.86.mid_ref), channel_id=1, source_target_pairs={{4,0},{8,4},{12,8},{5,1},{9,5},{13,9},{6,2},{10,6},{14,10},{7,3},{... | collective-permute-start | bytes 196616 | tf_op jit(solution)/shard_map/ppermute | solution.py:243
  32.3 1.4 %collective-permute-done.7.wx_l = f32[64,16,128]{2,1,0:T(8,128)S(1)} collective-permute-done((f32[64,16,128]{2,1,0:T(8,128)S(1)}, f32[64,16,128]{2,1,0:T(8,128)S(1)}, u32[]{:S(2)}, u32[]{:S(2)}) %collective-permute-start.7) | collective-permute-done | bytes 524320 | tf_op jit(solution)/shard_map/ppermute | solution.py:242
  33.6 4.4 %collective-permute-done.8.wx_r = f32[64,16,128]{2,1,0:T(8,128)S(1)} collective-permute-done((f32[64,16,128]{2,1,0:T(8,128)S(1)}, f32[64,16,128]{2,1,0:T(8,128)S(1)}, u32[]{:S(2)}, u32[]{:S(2)}) %collective-permute-start.8) | collective-permute-done | bytes 524320 | tf_op jit(solution)/shard_map/ppermute | solution.py:243
  38.0 23.5 %near.1 = f32[4,16,4,128]{3,2,1,0:T(4,128)} custom-call(s32[16,34]{1,0:T(8,128)S(1)} %add_add_fusion.list_ref, f32[64,8,128]{2,1,0:T(8,128)S(1)} %collective-permute-done.2.co_l, f32[64,8,128]{2,1,0:T(8,128)S(1)} %pad.4.co_m, f32[64,8,128]{2,1,0:T(8,128)S(1)} %collective-permute-done.3.co_r, f32[64,16,128]{2,1,0:T(8,128)S(1)} %collective-permute-done.7.wx_l, ...), custom_call_target="tpu_custom_call" | custom-call | flops 10000000000 | bytes 100000000 | tf_op jit(solution)/shard_map/near/pallas_call | solution.py:323
  61.5 3.5 %all-to-all-start = ((f32[4,16,4,128]{3,2,1,0:T(4,128)}), f32[4,16,4,128]{3,2,1,0:T(4,128)S(1)}, u32[]{:S(2)}, u32[]{:S(2)}) async-start(f32[4,16,4,128]{3,2,1,0:T(4,128)} %near.1), calls=%async_computation | async-start | bytes 262144 | tf_op jit(solution)/shard_map/all_to_all | solution.py:337
  65.1 32.5 %far.1 = f32[4,8192]{1,0:T(4,128)S(1)} custom-call(f32[64,256]{1,0:T(8,128)S(1)} %collective-permute-done.left_ref, f32[64,256]{1,0:T(8,128)S(1)} %reshape.86.mid_ref, f32[64,256]{1,0:T(8,128)S(1)} %collective-permute-done.1.right_ref, f32[8,64,64]{2,1,0:T(8,128)S(1)} %copy-done.3, f32[64,64,316]{2,1,0:T(8,128)} %bitcast.22, s32[64,316]{1,0:T(8,128)S(1)} %copy-done.4, ...), custom_call_target="tpu_custom_call" | custom-call | flops 10000000000 | bytes 100000000 | tf_op jit(solution)/shard_map/far/pallas_call | solution.py:286
  97.6 0.7 add.63
  (31 shorter events, 0.8 us)
Async XLA Ops:
  1.7 20.1 %collective-permute-start.4 = (f32[64,4,128]{2,1,0:T(4,128)S(1)}, f32[64,4,128]{2,1,0:T(4,128)S(1)}, u32[]{:S(2)}, u32[]{:S(2)}) collective-permute-start(f32[64,4,128]{2,1,0:T(4,128)S(1)} %broadcast_multiply_fusion), channel_id=1, source_target_pairs={{0,1},{1,2},{2,3},{3,0},{4,5},{5,6},{6,7},{7,4},{8,9},{9,10},{10,1... | collective-permute-start | bytes 393224 | tf_op jit(solution)/shard_map/ppermute | solution.py:264
  3.9 21.6 %collective-permute-start.5 = (f32[64,4,128]{2,1,0:T(4,128)S(1)}, f32[64,4,128]{2,1,0:T(4,128)S(1)}, u32[]{:S(2)}, u32[]{:S(2)}) collective-permute-start(f32[64,4,128]{2,1,0:T(4,128)S(1)} %broadcast_multiply_fusion), channel_id=1, source_target_pairs={{0,2},{1,3},{2,0},{3,1},{4,6},{5,7},{6,4},{7,5},{8,10},{9,11},{10,... | collective-permute-start | bytes 393224 | tf_op jit(solution)/shard_map/ppermute | solution.py:264
  6.2 19.3 %collective-permute-start.6 = (f32[64,4,128]{2,1,0:T(4,128)S(1)}, f32[64,4,128]{2,1,0:T(4,128)S(1)}, u32[]{:S(2)}, u32[]{:S(2)}) collective-permute-start(f32[64,4,128]{2,1,0:T(4,128)S(1)} %broadcast_multiply_fusion), channel_id=1, source_target_pairs={{0,3},{1,0},{2,1},{3,2},{4,7},{5,4},{6,5},{7,6},{8,11},{9,8},{10,9... | collective-permute-start | bytes 393224 | tf_op jit(solution)/shard_map/ppermute | solution.py:264
  8.2 22.0 %collective-permute-start.2 = (f32[64,8,128]{2,1,0:T(8,128)S(1)}, f32[64,8,128]{2,1,0:T(8,128)S(1)}, u32[]{:S(2)}, u32[]{:S(2)}) collective-permute-start(f32[64,8,128]{2,1,0:T(8,128)S(1)} %pad.4.co_m), channel_id=1, source_target_pairs={{0,4},{4,8},{8,12},{1,5},{5,9},{9,13},{2,6},{6,10},{10,14},{3,7},{... | collective-permute-start | bytes 786440 | tf_op jit(solution)/shard_map/ppermute | solution.py:242
  12.7 19.5 %collective-permute-start.3 = (f32[64,8,128]{2,1,0:T(8,128)S(1)}, f32[64,8,128]{2,1,0:T(8,128)S(1)}, u32[]{:S(2)}, u32[]{:S(2)}) collective-permute-start(f32[64,8,128]{2,1,0:T(8,128)S(1)} %pad.4.co_m), channel_id=1, source_target_pairs={{4,0},{8,4},{12,8},{5,1},{9,5},{13,9},{6,2},{10,6},{14,10},{7,3},{... | collective-permute-start | bytes 786440 | tf_op jit(solution)/shard_map/ppermute | solution.py:243
  15.8 1.6 %copy-start = (f32[64,64,128]{2,1,0:T(8,128)S(1)}, f32[64,64,128]{2,1,0:T(8,128)}, u32[]{:S(2)}) copy-start(f32[64,64,128]{2,1,0:T(8,128)} %basis_ref.3) | copy-start | bytes 6291460
  17.4 0.9 copy-start.2
  21.8 43.2 %collective-permute-start = (f32[64,256]{1,0:T(8,128)S(1)}, f32[64,256]{1,0:T(8,128)S(1)}, u32[]{:S(2)}, u32[]{:S(2)}) collective-permute-start(f32[64,256]{1,0:T(8,128)S(1)} %reshape.86.mid_ref), channel_id=1, source_target_pairs={{0,4},{4,8},{8,12},{1,5},{5,9},{9,13},{2,6},{6,10},{10,14},{3,7},{... | collective-permute-start | bytes 196616 | tf_op jit(solution)/shard_map/ppermute | solution.py:242
  25.6 8.0 %collective-permute-start.7 = (f32[64,16,128]{2,1,0:T(8,128)S(1)}, f32[64,16,128]{2,1,0:T(8,128)S(1)}, u32[]{:S(2)}, u32[]{:S(2)}) collective-permute-start(f32[64,16,128]{2,1,0:T(8,128)S(1)} %pad_maximum_fusion.wx_m), channel_id=1, source_target_pairs={{0,4},{4,8},{8,12},{1,5},{5,9},{9,13},{2,6},{6,10},{10,14},{3,7},{... | collective-permute-start | bytes 1572872 | tf_op jit(solution)/shard_map/ppermute | solution.py:242
  27.5 10.5 %collective-permute-start.8 = (f32[64,16,128]{2,1,0:T(8,128)S(1)}, f32[64,16,128]{2,1,0:T(8,128)S(1)}, u32[]{:S(2)}, u32[]{:S(2)}) collective-permute-start(f32[64,16,128]{2,1,0:T(8,128)S(1)} %pad_maximum_fusion.wx_m), channel_id=1, source_target_pairs={{4,0},{8,4},{12,8},{5,1},{9,5},{13,9},{6,2},{10,6},{14,10},{7,3},{... | collective-permute-start | bytes 1572872 | tf_op jit(solution)/shard_map/ppermute | solution.py:243
  30.2 34.9 %copy-start.1 = (f32[64,64,128]{2,1,0:T(8,128)S(1)}, f32[64,64,128]{2,1,0:T(8,128)}, u32[]{:S(2)}) copy-start(f32[64,64,128]{2,1,0:T(8,128)} %basis_ref.3) | copy-start | bytes 6291460
  30.2 34.9 %copy-start.3 = (f32[8,64,64]{2,1,0:T(8,128)S(1)}, f32[8,64,64]{2,1,0:T(8,128)}, u32[]{:S(2)}) copy-start(f32[8,64,64]{2,1,0:T(8,128)} %transfer_ref.1) | copy-start | bytes 393220
  30.2 34.9 %copy-start.4 = (s32[64,316]{1,0:T(8,128)S(1)}, s32[64,316]{1,0:T(8,128)}, u32[]{:S(2)}) copy-start(s32[64,316]{1,0:T(8,128)} %leaf_ref.1) | copy-start | bytes 242692
  30.2 34.9 %copy-start.5 = (s32[8,316]{1,0:T(8,128)S(1)}, s32[8,316]{1,0:T(8,128)}, u32[]{:S(2)}) copy-start(s32[8,316]{1,0:T(8,128)} %parent_ref.1) | copy-start | bytes 30340
  30.2 34.8 %collective-permute-start.1 = (f32[64,256]{1,0:T(8,128)S(1)}, f32[64,256]{1,0:T(8,128)S(1)}, u32[]{:S(2)}, u32[]{:S(2)}) collective-permute-start(f32[64,256]{1,0:T(8,128)S(1)} %reshape.86.mid_ref), channel_id=1, source_target_pairs={{4,0},{8,4},{12,8},{5,1},{9,5},{13,9},{6,2},{10,6},{14,10},{7,3},{... | collective-permute-start | bytes 196616 | tf_op jit(solution)/shard_map/ppermute | solution.py:243
  61.5 36.1 %all-to-all-start = ((f32[4,16,4,128]{3,2,1,0:T(4,128)}), f32[4,16,4,128]{3,2,1,0:T(4,128)S(1)}, u32[]{:S(2)}, u32[]{:S(2)}) async-start(f32[4,16,4,128]{3,2,1,0:T(4,128)} %near.1), calls=%async_computation | async-start | bytes 262144 | tf_op jit(solution)/shard_map/all_to_all | solution.py:337
